TPU v7x, 256 devices: a whole 4x4x8 slice. The times are simulated.
256 devices in a mesh: tr: 16 (over x_hi, z), tc: 16 (over y, x_lo, core).
Axes of the slice: x: 4 (x_hi: 2, x_lo: 2; x = x_hi * 2 + x_lo), y: 4, z: 8, core: 2. Of those that a mesh axis runs over, the one named last changes fastest.
Arguments:
- diag_block: bfloat16 [16, 16, 1024, 1024], P('tr', 'tc'), as said below
- coupling: bfloat16 [16, 16, 1024, 1024], P('tr', 'tc'), may hold values from -0.09375 to 0.09375
- precond: float32 [16, 16, 1024, 1024], P('tr', 'tc'), as said below
- rhs: float32 [16, 16, 1024, 128], P('tr', 'tc')
- slot_time: int32 [16, 16], P('tr', 'tc'), may hold values from 0 to 255, as said below
Outputs:
- solution: float32 [16, 16, 1024, 128], P('tr', 'tc')
- residual_norm: float32 [128], replicated
Inputs may be any that keep to these rules, and one draw needn't show every extreme that they name: `slot_time`: a permutation of the time blocks in which time blocks t and t + 1 always sit in slots adjacent along tr or along tc. `diag_block`: every block is symmetric and indefinite. `precond`: every block is symmetric positive definite.
All inputs are finite; a program needn't handle non-finite values.
Results may differ from a plain program's by a relative error of at most 0.0035.
Values may be sent and summed in bfloat16 or wider, within the bound.
No kernel may reach another device: no remote copies, remote signals or barrier semaphores. Data moves between devices by JAX's collectives and lax.ppermute only.
A program may use at most 128 MiB of HBM per device.

v0:
```python
import functools

import jax
import jax.numpy as jnp
from jax import lax
from jax.experimental import pallas as pl
from jax.experimental.pallas import tpu as pltpu
from jax.sharding import PartitionSpec as P

ITERS = 3
BASIS = ITERS + 1
PAIRS = tuple((i, j) for i in range(BASIS) for j in range(i, BASIS))
LEAF = 256
SLOTS = 16
F32 = jnp.float32
BF16 = jnp.bfloat16
MIB = 2**20


def vmem():
    return pl.BlockSpec(memory_space=pltpu.VMEM)


def smem():
    return pl.BlockSpec(memory_space=pltpu.SMEM)


def pinned(x, space=pltpu.VMEM):
    return pltpu.with_memory_space_constraint(x, space)


def params(mib):
    return pltpu.CompilerParams(vmem_limit_bytes=mib * MIB)


def mm(a, b):
    return lax.dot_general(a, b, (((1,), (0,)), ((), ())), preferred_element_type=F32)


def tn(a, b):
    return lax.dot_general(a, b, (((0,), (0,)), ((), ())), preferred_element_type=F32)


def split(x):
    high = x.astype(BF16)
    return high, (x - high.astype(F32)).astype(BF16)


def mm3(a, b):
    return mm(a[0], b[0]) + (mm(a[0], b[1]) + mm(a[1], b[0]))


def tn3(a, b):
    return tn(a[0], b[0]) + (tn(a[0], b[1]) + tn(a[1], b[0]))


def mm_full(a, b):
    return lax.dot_general(a, b, (((1,), (0,)), ((), ())), precision=lax.Precision.HIGHEST)


def tn_full(a, b):
    return lax.dot_general(a, b, (((0,), (0,)), ((), ())), precision=lax.Precision.HIGHEST)


def column_norm(x):
    return jnp.max(jnp.sum(jnp.abs(x), axis=0, keepdims=True), axis=1, keepdims=True)


def pivot_steps(block):
    n = block.shape[0]
    rows = lax.broadcasted_iota(jnp.int32, (n, n), 0)
    cols = lax.broadcasted_iota(jnp.int32, (n, n), 1)
    eye = jnp.where(rows == cols, 1.0, 0.0).astype(F32)
    diag = jnp.where(rows == cols, block, 0.0)
    across = lax.rsqrt(jnp.sum(diag, axis=0, keepdims=True))
    down = lax.rsqrt(jnp.sum(diag, axis=1, keepdims=True))
    scaled = block * down * across
    parts = split(scaled)
    square = mm(parts[0], parts[0])
    yield
    alpha = 1.8 * lax.rsqrt(column_norm(square))
    power = (eye - (2.0 * alpha) * scaled + (alpha * alpha) * square).astype(BF16)
    inv = alpha * (2.0 * eye - alpha * scaled)
    for _ in range(2):
        inv = inv + mm(inv.astype(BF16), power)
        power = mm(power, power).astype(BF16)
        yield
    inv = inv + mm(inv.astype(BF16), power)
    yield
    high = inv.astype(BF16)
    resid = eye - (mm(parts[0], high) + mm(parts[1], high))
    yield
    inv = high.astype(F32) + mm(high, resid.astype(BF16))
    yield
    inv_parts = split(inv)
    resid = eye - mm3(parts, inv_parts)
    yield
    inv = inv + mm(inv_parts[0], resid.astype(BF16))
    error = column_norm(resid)
    return inv * down * across, error


def interleave(steps, pending):
    while True:
        try:
            next(steps)
        except StopIteration as stop:
            return stop.value
        if pending:
            pending.pop(0)()


def eliminate(n, work, vec, extra, before, after):
    blocks = n // LEAF
    at = [pl.ds(k * LEAF, LEAF) for k in range(blocks)]
    worst = jnp.zeros((1, 1), F32)
    pending = []
    for k in range(blocks):
        before(k)
        pivot, error = interleave(pivot_steps(work[at[k], at[k]]), pending)
        for task in pending:
            task()
        after(k)
        worst = jnp.maximum(worst, error)
        parts = split(pivot)
        work[at[k], at[k]] = pivot
        old, row = {}, {}

        def scale_row(j, k=k, old=old, row=row, parts=parts):
            old[j] = split(work[at[k], at[j]])
            value = mm3(parts, old[j])
            row[j] = split(value)
            work[at[k], at[j]] = value

        def update(i, j, old=old, row=row):
            work[at[i], at[j]] = work[at[i], at[j]] - tn3(old[i], row[j])

        def push(i, k=k, row=row):
            vec[at[i], :] = vec[at[i], :] - tn3(row[i], split(vec[at[k], :]))

        def solve(k=k, parts=parts):
            vec[at[k], :] = mm3(parts, split(vec[at[k], :]))

        pending = []
        later = range(k + 1, blocks)
        for j in later:
            if j == k + 1:
                scale_row(j)
                update(j, j)
            else:
                pending.append(functools.partial(scale_row, j))
        for i in later:
            for j in range(i, blocks):
                if (i, j) != (k + 1, k + 1):
                    pending.append(functools.partial(update, i, j))
        for i in later:
            pending.append(functools.partial(push, i))
        pending.append(solve)
        pending += extra(k)
    for task in pending:
        task()
    for k in reversed(range(blocks - 1)):
        total = vec[at[k], :]
        for j in range(k + 1, blocks):
            total = total - mm3(split(work[at[k], at[j]]), split(vec[at[j], :]))
        vec[at[k], :] = total
    return worst


def careful_inverse(block):
    n = block.shape[0]
    rows = lax.broadcasted_iota(jnp.int32, (n, n), 0)
    cols = lax.broadcasted_iota(jnp.int32, (n, n), 1)
    eye = jnp.where(rows == cols, 1.0, 0.0).astype(F32)
    diag = jnp.where(rows == cols, block, 0.0)
    across = lax.rsqrt(jnp.sum(diag, axis=0, keepdims=True))
    down = lax.rsqrt(jnp.sum(diag, axis=1, keepdims=True))
    scaled = block * down * across

    def unfinished(carry):
        return jnp.logical_and(carry[2] > 1e-3, carry[0] < 80)

    def refine(carry):
        count, x, _ = carry
        left = eye - mm_full(scaled, x)
        return count + 1, x + mm_full(x, left), jnp.max(column_norm(left))

    start = eye * (1.8 / column_norm(scaled))
    return lax.while_loop(unfinished, refine, (jnp.int32(0), start, jnp.float32(2.0)))[1] * down * across


def eliminate_careful(n, work, vec, row):
    blocks = n // LEAF

    def at(k):
        return pl.ds(pl.multiple_of(k * LEAF, LEAF), LEAF)

    def pivot(k, _):
        work[at(k), at(k)] = careful_inverse(work[at(k), at(k)])

        def scale_row(j, _):
            row[:, at(j)] = mm_full(work[at(k), at(k)], work[at(k), at(j)])
            return 0

        def update_row(i, _):
            def update(j, _):
                work[at(i), at(j)] = work[at(i), at(j)] - tn_full(work[at(k), at(i)], row[:, at(j)])
                return 0

            lax.fori_loop(i, blocks, update, 0)
            vec[at(i), :] = vec[at(i), :] - tn_full(row[:, at(i)], vec[at(k), :])
            return 0

        def keep(j, _):
            work[at(k), at(j)] = row[:, at(j)]
            return 0

        lax.fori_loop(k + 1, blocks, scale_row, 0)
        lax.fori_loop(k + 1, blocks, update_row, 0)
        lax.fori_loop(k + 1, blocks, keep, 0)
        vec[at(k), :] = mm_full(work[at(k), at(k)], vec[at(k), :])
        return 0

    def back(m, _):
        k = blocks - 2 - m

        def subtract(j, _):
            vec[at(k), :] = vec[at(k), :] - mm_full(work[at(k), at(j)], vec[at(j), :])
            return 0

        return lax.fori_loop(k + 1, blocks, subtract, 0)

    lax.fori_loop(0, blocks, pivot, 0)
    lax.fori_loop(0, blocks - 1, back, 0)


def factor_kernel(own, t0, t1, t2, t3, p_hbm, rhs_hbm, c_hbm, d_hbm, work, c_ref, ct_ref, d_ref, rhs_ref, vec, flags, m0, m1, m2, m3, row, times, sems, time_sems):
    n = work.shape[0]
    blocks = n // LEAF
    first = pl.ds(0, LEAF)
    rest = pl.ds(LEAF, n - LEAF)
    spots = [(first, first), (first, rest)] + [(pl.ds(k * LEAF, LEAF), pl.ds(0, n)) for k in range(1, blocks)]
    panels = [pltpu.make_async_copy(p_hbm.at[spot], work.at[spot], sems.at[k]) for k, spot in enumerate(spots)]
    others = [
        pltpu.make_async_copy(src, dst, sems.at[len(spots) + i])
        for i, (src, dst) in enumerate(((rhs_hbm, rhs_ref), (c_hbm, c_ref), (d_hbm, d_ref)))
    ]
    known = [pltpu.make_async_copy(t, times.at[pl.ds(d, 1), :], time_sems.at[d]) for d, t in enumerate((own, t0, t1, t2, t3))]

    def before(k):
        if k == 0:
            panels[0].start()
            panels[0].wait()
            for copy in panels[1:] + others + known:
                copy.start()
        elif k == 1:
            others[1].wait()

    def after(k):
        if k == 0:
            for copy in panels[1:]:
                copy.wait()
            others[0].wait()
            vec[...] = rhs_ref[...]

    def flip(k):
        ct_ref[:, pl.ds(k * LEAF, LEAF)] = c_ref[pl.ds(k * LEAF, LEAF), :].T

    def extra(k):
        if k == 0:
            return []
        if k == blocks - 1:
            return []
        span = blocks // 2
        return [functools.partial(flip, j) for j in range((k - 1) * span, k * span)]

    worst = eliminate(n, work, vec, extra, before, after)

    @pl.when(jnp.logical_not(jnp.max(worst) < 5e-3))
    def _():
        for copy in panels:
            copy.start()
        for copy in panels:
            copy.wait()
        vec[...] = rhs_ref[...]
        eliminate_careful(n, work, vec, row)

    others[2].wait()
    for copy in known:
        copy.wait()
    here = times[0, 0]
    for d in range(4):
        flags[0, d] = (times[1 + d, 0] == here + 1).astype(jnp.int32)
        flags[0, 4 + d] = (times[1 + d, 0] == here - 1).astype(jnp.int32)
    write_messages(flags, ct_ref, vec, (m0, m1, m2, m3))


def factor(tags, precond, rhs, coupling, diag):
    n, width = rhs.shape
    square = pltpu.VMEM((n, n), BF16)
    column = pltpu.VMEM((n, width), F32)
    outside = pl.BlockSpec(memory_space=pltpu.HBM)
    return pl.pallas_call(
        factor_kernel,
        out_shape=[pltpu.VMEM((n, n), F32), square, square, square, column, column, pltpu.SMEM((1, 8), jnp.int32)]
        + [jax.ShapeDtypeStruct((n, width), BF16)] * 4,
        in_specs=[outside] * 9,
        out_specs=[vmem()] * 6 + [smem()] + [vmem()] * 4,
        scratch_shapes=[
            pltpu.VMEM((LEAF, n), F32),
            pltpu.SMEM((8, 1), jnp.int32),
            pltpu.SemaphoreType.DMA((n // LEAF + 4,)),
            pltpu.SemaphoreType.DMA((5,)),
        ],
        compiler_params=params(20),
    )(*[pinned(x, pltpu.HBM) for x in (*tags, precond, rhs, coupling, diag)])


def build_kernel(work, high_ref, low_ref, size_ref):
    n = work.shape[0]
    blocks = n // LEAF
    at = [pl.ds(k * LEAF, LEAF) for k in range(blocks)]
    inv = {}
    largest = jnp.zeros((1, 1), F32)
    for k in reversed(range(blocks)):
        row = {j: split(work[at[k], at[j]]) for j in range(k + 1, blocks)}
        made = {}
        for j in range(k + 1, blocks):
            made[j] = -sum(mm3(row[m], inv[m, j]) for m in range(k + 1, blocks))
            inv[k, j] = split(made[j])
            flipped = made[j].T
            inv[j, k] = split(flipped)
        made[k] = work[at[k], at[k]] - sum([mm3(row[m], inv[m, k]) for m in range(k + 1, blocks)])
        inv[k, k] = split(made[k])
        for j in range(k, blocks):
            high_ref[at[k], at[j]], low_ref[at[k], at[j]] = inv[k, j]
            if j != k:
                high_ref[at[j], at[k]], low_ref[at[j], at[k]] = inv[j, k]
            largest = jnp.maximum(largest, jnp.max(jnp.max(jnp.abs(made[j]), axis=0, keepdims=True), axis=1, keepdims=True))
    size_ref[...] = jnp.broadcast_to(largest, size_ref.shape)


def build(work, width):
    n = work.shape[0]
    return pl.pallas_call(
        build_kernel,
        out_shape=[pltpu.VMEM((n, n), BF16), pltpu.VMEM((n, n), BF16), pltpu.VMEM((8, width), F32)],
        in_specs=[vmem()],
        out_specs=[vmem()] * 3,
        compiler_params=params(16),
    )(pinned(work))


def store_applied(out_ref, high_ref, low_ref, vec_ref):
    high, low = split(vec_ref[...])
    both = jnp.concatenate([high, low], axis=1)
    width = high.shape[1]
    for k in range(0, out_ref.shape[0], LEAF):
        rows = pl.ds(k, LEAF)
        part = mm(high_ref[rows, :], both)
        out_ref[rows, :] = part[:, :width] + (part[:, width:] + mm(low_ref[rows, :], high))


def relation(flags):
    return [flags[0, d] == 1 for d in range(4)], [flags[0, 4 + d] == 1 for d in range(4)]


def write_messages(flags, ct_ref, vec_ref, out_refs):
    is_next, is_prev = relation(flags)
    high = vec_ref[...].astype(BF16)
    for k in range(0, vec_ref.shape[0], LEAF):
        rows = pl.ds(k, LEAF)
        back = mm(ct_ref[rows, :], high).astype(BF16)
        ahead = high[k:k + LEAF, :]
        for d, out in enumerate(out_refs):
            out[rows, :] = jnp.where(is_next[d], ahead, jnp.where(is_prev[d], back, jnp.zeros_like(back)))


def own_kernel(diag_ref, vec_ref, out_ref):
    both = jnp.concatenate(split(vec_ref[...]), axis=1)
    width = vec_ref.shape[1]
    for k in range(0, out_ref.shape[0], LEAF):
        rows = pl.ds(k, LEAF)
        part = mm(diag_ref[rows, :], both)
        out_ref[rows, :] = part[:, :width] + part[:, width:]


def residual_rows(flags, own_ref, c_ref, got, out_ref):
    is_next, is_prev = relation(flags)
    zero = jnp.zeros(got[0].shape, BF16)
    before = zero
    for d, ref in enumerate(got):
        before = jnp.where(is_prev[d], ref[...], before)
    for k in range(0, out_ref.shape[0], LEAF):
        rows = pl.ds(k, LEAF)
        after = zero[:LEAF]
        for d, ref in enumerate(got):
            after = jnp.where(is_next[d], ref[rows, :], after)
        out_ref[rows, :] = own_ref[rows, :] + mm(c_ref[rows, :], before) + after.astype(F32)


def step_kernel(flags, own_ref, c_ref, ct_ref, high_ref, low_ref, g0, g1, g2, g3, res_ref, vec_ref, *out_refs):
    residual_rows(flags, own_ref, c_ref, (g0, g1, g2, g3), res_ref)
    store_applied(vec_ref, high_ref, low_ref, res_ref)
    write_messages(flags, ct_ref, vec_ref, out_refs)


def pack(rows, out_ref):
    rows = rows + [jnp.zeros_like(rows[0])] * (SLOTS - len(rows))
    packed = jnp.concatenate(rows, axis=0)
    for d in range(0, out_ref.shape[0], SLOTS):
        out_ref[pl.ds(d, SLOTS), :] = packed


def last_kernel(flags, own_ref, c_ref, high_ref, low_ref, size_ref, r0, p0, r1, p1, r2, p2, g0, g1, g2, g3, out_ref, r3, p3):
    residual_rows(flags, own_ref, c_ref, (g0, g1, g2, g3), r3)
    store_applied(p3, high_ref, low_ref, r3)
    res = (r0, r1, r2, r3)
    vec = (p0, p1, p2, p3)
    unit = size_ref[0:1, :]
    sizes = [jnp.maximum(jnp.max(jnp.abs(r[...]), axis=0, keepdims=True), 1e-30) for r in res]
    left_scale = [1.0 / v for v in sizes]
    right_scale = [1.0 / (v * unit) for v in sizes]
    rows = [jnp.zeros_like(unit)] * len(PAIRS)
    for k in range(0, r3.shape[0], LEAF):
        at = pl.ds(k, LEAF)
        left = [res[i][at, :] * left_scale[i] for i in range(BASIS)]
        right = [vec[i][at, :] * right_scale[i] for i in range(BASIS)]
        for m, (i, j) in enumerate(PAIRS):
            rows[m] = rows[m] + jnp.sum(left[i] * right[j], axis=0, keepdims=True)
    pack(rows + sizes + [unit], out_ref)


def merge(in_ref):
    senders = in_ref.shape[0] // SLOTS
    got = [in_ref[pl.ds(m, senders, stride=SLOTS), :] for m in range(len(PAIRS) + BASIS + 1)]
    size_rows, unit_row = got[len(PAIRS):-1], got[-1]
    sizes = [jnp.max(v, axis=0, keepdims=True) for v in size_rows]
    unit = jnp.max(unit_row, axis=0, keepdims=True)
    share = [v / top for v, top in zip(size_rows, sizes)]
    unit_share = unit_row / unit
    rows = []
    for m, (i, j) in enumerate(PAIRS):
        rows.append(jnp.sum(got[m] * (share[i] * share[j] * unit_share), axis=0, keepdims=True))
    return rows, sizes, unit


def merge_kernel(in_ref, out_ref):
    rows, sizes, unit = merge(in_ref)
    pack(rows + sizes + [unit], out_ref)


def recurrence(rows, sizes, unit):
    gram = {}
    for m, (i, j) in enumerate(PAIRS):
        gram[i, j] = gram[j, i] = rows[m]
    lead = sizes[1] / sizes[0]
    grow = [sizes[j + 1] / sizes[j] / lead for j in range(ITERS)]
    zero = jnp.zeros_like(unit)

    def dot(a, b):
        return sum(a[i] * b[j] * gram[i, j] for i in a for j in b)

    def axpy(a, x, y):
        out = {i: a * v for i, v in x.items()}
        for i, v in y.items():
            out[i] = out[i] + v if i in out else v
        return out

    resid_new = {0: jnp.ones_like(unit)}
    resid_old = {}
    beta_now = jnp.sqrt(dot(resid_new, resid_new))
    old_beta = zero
    phi_bar = beta_now
    cosine = -jnp.ones_like(unit)
    sine_now = eps_now = d_bar = zero
    dir_now, dir_old, total = {}, {}, {}
    for step in range(ITERS):
        lanczos = {i: v / beta_now for i, v in resid_new.items()}
        image = {i + 1: v * grow[i] for i, v in lanczos.items()}
        if step > 0:
            image = axpy(-beta_now / old_beta, resid_old, image)
        alpha_now = dot(lanczos, image)
        resid_old = resid_new
        resid_new = axpy(-alpha_now / beta_now, resid_new, image)
        old_beta = beta_now
        beta_now = jnp.sqrt(dot(resid_new, resid_new))
        old_eps = eps_now
        delta_now = cosine * d_bar + sine_now * alpha_now
        g_bar = sine_now * d_bar - cosine * alpha_now
        eps_now = sine_now * beta_now
        d_bar = -cosine * beta_now
        gamma_now = jnp.sqrt(g_bar * g_bar + beta_now * beta_now)
        cosine = g_bar / gamma_now
        sine_now = beta_now / gamma_now
        phi_now = cosine * phi_bar
        phi_bar = sine_now * phi_bar
        dir_next = axpy(-old_eps, dir_old, axpy(-delta_now, dir_now, lanczos))
        dir_next = {i: v / gamma_now for i, v in dir_next.items()}
        dir_old, dir_now = dir_now, dir_next
        total = axpy(phi_now, dir_now, total)
    coefs = [total[i] * (sizes[0] / sizes[i]) / lead for i in range(ITERS)]
    return coefs, phi_bar * sizes[0] * jnp.sqrt(unit)


def finish_kernel(in_ref, p0, p1, p2, out_ref, norm_ref):
    coefs, norm = recurrence(*merge(in_ref))
    norm_ref[...] = norm
    for k in range(0, out_ref.shape[0], LEAF):
        at = pl.ds(k, LEAF)
        out_ref[at, :] = coefs[0] * p0[at, :] + coefs[1] * p1[at, :] + coefs[2] * p2[at, :]


def neighbour_perms(count):
    even = [(i, i ^ 1) for i in range(count)]
    odd = [(i, i + 1) for i in range(1, count - 1, 2)]
    return even, odd + [(j, i) for i, j in odd]


def exchange(values):
    even_r, odd_r = neighbour_perms(lax.axis_size("tr"))
    even_c, odd_c = neighbour_perms(lax.axis_size("tc"))
    return [
        lax.ppermute(values[0], "tr", odd_r),
        lax.ppermute(values[1], "tc", odd_c),
        lax.ppermute(values[2], "tr", even_r),
        lax.ppermute(values[3], "tc", even_c),
    ]


def body(diag_block, coupling, precond, rhs, slot_time):
    n, width = rhs.shape[2:]
    own_tag = slot_time + 1
    tags = [own_tag] + exchange([own_tag] * 4)
    sent = [jax.ShapeDtypeStruct((n, width), BF16)] * 4

    work, c_here, flipped, diag_here, res, vec, flags, *messages = factor(
        tags, precond[0, 0], rhs[0, 0], coupling[0, 0], diag_block[0, 0]
    )
    basis = [res, vec]
    for step in range(ITERS):
        got = exchange(messages)
        if step == 0:
            high, low, size = build(work, width)
        own = pl.pallas_call(
            own_kernel,
            out_shape=pltpu.VMEM((n, width), F32),
            in_specs=[vmem()] * 2,
            out_specs=vmem(),
            compiler_params=params(8),
        )(pinned(diag_here), pinned(vec))
        if step < ITERS - 1:
            out = pl.pallas_call(
                step_kernel,
                out_shape=[pltpu.VMEM((n, width), F32)] * 2 + sent,
                in_specs=[smem()] + [vmem()] * 9,
                out_specs=[vmem()] * 6,
                compiler_params=params(12),
            )(pinned(flags, pltpu.SMEM), pinned(own), pinned(c_here), pinned(flipped), pinned(high), pinned(low), *got)
            vec = out[1]
            basis += [out[0], vec]
            messages = out[2:]
    part = pl.pallas_call(
        last_kernel,
        out_shape=jax.ShapeDtypeStruct((lax.axis_size("tc") * SLOTS, width), F32),
        in_specs=[smem()] + [vmem()] * 15,
        out_specs=vmem(),
        scratch_shapes=[pltpu.VMEM((n, width), F32)] * 2,
        compiler_params=params(12),
    )(pinned(flags, pltpu.SMEM), pinned(own), pinned(c_here), pinned(high), pinned(low), pinned(size), *[pinned(b) for b in basis], *got)
    part = lax.all_to_all(part, "tc", 0, 0, tiled=True)
    part = pl.pallas_call(
        merge_kernel,
        out_shape=jax.ShapeDtypeStruct((lax.axis_size("tr") * SLOTS, width), F32),
        in_specs=[vmem()],
        out_specs=vmem(),
    )(part)
    part = lax.all_to_all(part, "tr", 0, 0, tiled=True)
    solution, norm = pl.pallas_call(
        finish_kernel,
        out_shape=[jax.ShapeDtypeStruct((n, width), F32), jax.ShapeDtypeStruct((1, width), F32)],
        in_specs=[vmem()] * 4,
        out_specs=[vmem()] * 2,
        compiler_params=params(8),
    )(part, pinned(basis[1]), pinned(basis[3]), pinned(basis[5]))
    return (solution[None, None], norm[0])


def solution(mesh):
    placed = (
        P("tr", "tc", None, None),
        P("tr", "tc", None, None),
        P("tr", "tc", None, None),
        P("tr", "tc", None, None),
        P("tr", "tc"),
    )
    return jax.shard_map(
        body,
        mesh=mesh,
        in_specs=placed,
        out_specs=(P("tr", "tc", None, None), P()),
        check_vma=False,
    )
```

profile of v0, /device:TPU:1, one launch (start us, length us, event | category | flops | bytes accessed | tf_op | source)
XLA Modules:
  0.0 121.1 jit_solution(12677329720534363803)
XLA Ops:
  1.3 4.1 %collective-permute-start.3 = (s32[1,1]{1,0:T(1,128)}, s32[1,1]{1,0:T(1,128)}, u32[]{:S(2)}, u32[]{:S(2)}) collective-permute-start(s32[1,1]{1,0:T(1,128)} %add.3.own), channel_id=1, source_target_pairs={{0,1},{1,0},{2,3},{3,2},{4,5},{5,4},{6,7},{7,6},{8,9},{9,8},{10,11... | collective-permute-start | bytes 20 | tf_op jit(solution)/shard_map/ppermute | solution.py:527
  5.4 0.7 collective-permute-start.2
  6.2 4.5 %collective-permute-start.1 = (s32[1,1]{1,0:T(1,128)}, s32[1,1]{1,0:T(1,128)}, u32[]{:S(2)}, u32[]{:S(2)}) collective-permute-start(s32[1,1]{1,0:T(1,128)} %add.3.own), channel_id=1, source_target_pairs={{1,2},{3,4},{5,6},{7,8},{9,10},{11,12},{13,14},{2,1},{4,3},{6,5},{... | collective-permute-start | bytes 20 | tf_op jit(solution)/shard_map/ppermute | solution.py:525
  10.6 1.2 collective-permute-start
  11.8 16.4 %shard_map.68 = (f32[1024,1024]{1,0:T(8,128)S(1)}, bf16[1024,1024]{1,0:T(8,128)(2,1)S(1)}, bf16[1024,1024]{1,0:T(8,128)(2,1)S(1)}, bf16[1024,1024]{1,0:T(8,128)(...) custom-call(s32[1,1]{1,0:T(1,128)} %add.3.own, ...), custom_call_target="tpu_custom_call" | custom-call | tf_op jit(solution)/shard_map/pallas_call | solution.py:303
  28.2 0.7 collective-permute-start.4
  28.9 3.1 %collective-permute-start.5 = (bf16[1024,128]{1,0:T(8,128)(2,1)S(1)}, bf16[1024,128]{1,0:T(8,128)(2,1)S(1)}, u32[]{:S(2)}, u32[]{:S(2)}) collective-permute-start(bf16[1024,128]{1,0:T(8,128)(2,1)S(1)} %get-tuple-element.39), channel_id=1, source_target_pairs={{1,2},{3,4},{5,6},{7,8},{9,10},{11,12},{13,14},{2,1},{4,3},{6,5},{... | collective-permute-start | bytes 786440 | tf_op jit(solution)/shard_map/ppermute | solution.py:525
  32.0 8.6 %collective-permute-start.6 = (bf16[1024,128]{1,0:T(8,128)(2,1)S(1)}, bf16[1024,128]{1,0:T(8,128)(2,1)S(1)}, u32[]{:S(2)}, u32[]{:S(2)}) collective-permute-start(bf16[1024,128]{1,0:T(8,128)(2,1)S(1)} %get-tuple-element.40), channel_id=1, source_target_pairs={{0,16},{16,0},{32,48},{48,32},{64,80},{80,64},{96,112},{112,96},{1... | collective-permute-start | bytes 786440 | tf_op jit(solution)/shard_map/ppermute | solution.py:526
  40.6 3.8 %shard_map.70 = (bf16[1024,1024]{1,0:T(8,128)(2,1)S(1)}, bf16[1024,1024]{1,0:T(8,128)(2,1)S(1)}, f32[8,128]{1,0:T(8,128)S(1)}) custom-call(f32[1024,1024]{1,0:T(8,128)S(1)} %get-tuple-element.35.work), custom_call_target="tpu_custom_call" | custom-call | tf_op jit(solution)/shard_map/pallas_call | solution.py:345
  44.4 0.7 shard_map.69.own_ref
  45.2 0.0 collective-permute-done.4.g0
  45.2 0.0 collective-permute-done.6.g2
  45.2 0.0 collective-permute-done.7.g3
  45.2 2.5 %shard_map.71 = (f32[1024,128]{1,0:T(8,128)S(1)}, f32[1024,128]{1,0:T(8,128)S(1)}, bf16[1024,128]{1,0:T(8,128)(2,1)S(1)}, bf16[1024,128]{1,0:T(8,128)(2,1)S(1)},...) custom-call(s32[1,8]{1,0:T(1,128)S(4)} %get-tuple-element.30.flags, f32[1024,128]{1,0:T(8,128)S(1)} %shard_map.69.own_ref, ...), custom_call_target="tpu_custom_call" | custom-call | tf_op jit(solution)/shard_map/pallas_call | solution.py:553
  47.7 0.7 collective-permute-start.8
  48.4 4.2 %collective-permute-start.9 = (bf16[1024,128]{1,0:T(8,128)(2,1)S(1)}, bf16[1024,128]{1,0:T(8,128)(2,1)S(1)}, u32[]{:S(2)}, u32[]{:S(2)}) collective-permute-start(bf16[1024,128]{1,0:T(8,128)(2,1)S(1)} %get-tuple-element.44), channel_id=1, source_target_pairs={{1,2},{3,4},{5,6},{7,8},{9,10},{11,12},{13,14},{2,1},{4,3},{6,5},{... | collective-permute-start | bytes 786440 | tf_op jit(solution)/shard_map/ppermute | solution.py:525
  52.6 6.4 %collective-permute-start.10 = (bf16[1024,128]{1,0:T(8,128)(2,1)S(1)}, bf16[1024,128]{1,0:T(8,128)(2,1)S(1)}, u32[]{:S(2)}, u32[]{:S(2)}) collective-permute-start(bf16[1024,128]{1,0:T(8,128)(2,1)S(1)} %get-tuple-element.45), channel_id=1, source_target_pairs={{0,16},{16,0},{32,48},{48,32},{64,80},{80,64},{96,112},{112,96},{1... | collective-permute-start | bytes 786440 | tf_op jit(solution)/shard_map/ppermute | solution.py:526
  59.0 0.0 collective-permute-start.11
  59.0 0.7 shard_map.72.own_ref
  59.7 3.0 %collective-permute-done.10.g2 = bf16[1024,128]{1,0:T(8,128)(2,1)S(1)} collective-permute-done((bf16[1024,128]{1,0:T(8,128)(2,1)S(1)}, bf16[1024,128]{1,0:T(8,128)(2,1)S(1)}, u32[]{:S(2)}, u32[]{:S(2)}) %collective-permute-start.10) | collective-permute-done | bytes 262176 | tf_op jit(solution)/shard_map/ppermute | solution.py:526
  62.8 2.5 %shard_map.73 = (f32[1024,128]{1,0:T(8,128)S(1)}, f32[1024,128]{1,0:T(8,128)S(1)}, bf16[1024,128]{1,0:T(8,128)(2,1)S(1)}, bf16[1024,128]{1,0:T(8,128)(2,1)S(1)},...) custom-call(s32[1,8]{1,0:T(1,128)S(4)} %get-tuple-element.30.flags, f32[1024,128]{1,0:T(8,128)S(1)} %shard_map.72.own_ref, ...), custom_call_target="tpu_custom_call" | custom-call | tf_op jit(solution)/shard_map/pallas_call | solution.py:553
  65.3 0.7 collective-permute-start.12
  66.0 3.6 %collective-permute-start.13 = (bf16[1024,128]{1,0:T(8,128)(2,1)S(1)}, bf16[1024,128]{1,0:T(8,128)(2,1)S(1)}, u32[]{:S(2)}, u32[]{:S(2)}) collective-permute-start(bf16[1024,128]{1,0:T(8,128)(2,1)S(1)} %get-tuple-element.53), channel_id=1, source_target_pairs={{1,2},{3,4},{5,6},{7,8},{9,10},{11,12},{13,14},{2,1},{4,3},{6,5},{... | collective-permute-start | bytes 786440 | tf_op jit(solution)/shard_map/ppermute | solution.py:525
  69.6 3.4 %collective-permute-start.14 = (bf16[1024,128]{1,0:T(8,128)(2,1)S(1)}, bf16[1024,128]{1,0:T(8,128)(2,1)S(1)}, u32[]{:S(2)}, u32[]{:S(2)}) collective-permute-start(bf16[1024,128]{1,0:T(8,128)(2,1)S(1)} %get-tuple-element.54), channel_id=1, source_target_pairs={{0,16},{16,0},{32,48},{48,32},{64,80},{80,64},{96,112},{112,96},{1... | collective-permute-start | bytes 786440 | tf_op jit(solution)/shard_map/ppermute | solution.py:526
  73.0 0.0 collective-permute-start.15
  73.0 0.7 shard_map.74.own_ref
  73.7 3.0 %collective-permute-done.14.g2 = bf16[1024,128]{1,0:T(8,128)(2,1)S(1)} collective-permute-done((bf16[1024,128]{1,0:T(8,128)(2,1)S(1)}, bf16[1024,128]{1,0:T(8,128)(2,1)S(1)}, u32[]{:S(2)}, u32[]{:S(2)}) %collective-permute-start.14) | collective-permute-done | bytes 262176 | tf_op jit(solution)/shard_map/ppermute | solution.py:526
  76.7 2.5 %shard_map.75 = f32[256,128]{1,0:T(8,128)S(1)} custom-call(s32[1,8]{1,0:T(1,128)S(4)} %get-tuple-element.30.flags, f32[1024,128]{1,0:T(8,128)S(1)} %shard_map.74.own_ref, bf16[1024,1024]{1,0:T(8,128)(2,1)S(1)} %get-tuple-element.33.c_ref, bf16[1024,1024]{1,0:T(8,128)(2,1)S(1)} %get-tuple-element.36.high_ref, ...), custom_call_target="tpu_custom_call" | custom-call | tf_op jit(solution)/shard_map/pallas_call | solution.py:563
  79.2 16.8 %all_to_all.22 = f32[16,16,128]{2,1,0:T(8,128)} all-to-all(f32[16,16,128]{2,1,0:T(8,128)S(1)} %bitcast.11), channel_id=1, replica_groups=mesh['tr'=16,'tc'=16] {'tc'}, dimensions={0} | all-to-all | bytes 262144 | tf_op jit(solution)/shard_map/all_to_all | solution.py:571
  96.0 1.6 %shard_map.76 = f32[256,128]{1,0:T(8,128)} custom-call(f32[256,128]{1,0:T(8,128)} %bitcast.16), custom_call_target="tpu_custom_call" | custom-call | tf_op jit(solution)/shard_map/pallas_call | solution.py:572
  97.6 22.5 %all_to_all.23 = f32[16,16,128]{2,1,0:T(8,128)S(1)} all-to-all(f32[16,16,128]{2,1,0:T(8,128)} %bitcast.17), channel_id=1, replica_groups=mesh['tr'=16,'tc'=16] {'tr'}, dimensions={0} | all-to-all | bytes 262144 | tf_op jit(solution)/shard_map/all_to_all | solution.py:578
  120.1 1.1 shard_map.77
  (12 shorter events, 0.0 us)
Async XLA Ops:
  1.3 10.5 %collective-permute-start.3 = (s32[1,1]{1,0:T(1,128)}, s32[1,1]{1,0:T(1,128)}, u32[]{:S(2)}, u32[]{:S(2)}) collective-permute-start(s32[1,1]{1,0:T(1,128)} %add.3.own), channel_id=1, source_target_pairs={{0,1},{1,0},{2,3},{3,2},{4,5},{5,4},{6,7},{7,6},{8,9},{9,8},{10,11... | collective-permute-start | bytes 20 | tf_op jit(solution)/shard_map/ppermute | solution.py:527
  5.4 6.4 %collective-permute-start.2 = (s32[1,1]{1,0:T(1,128)}, s32[1,1]{1,0:T(1,128)}, u32[]{:S(2)}, u32[]{:S(2)}) collective-permute-start(s32[1,1]{1,0:T(1,128)} %add.3.own), channel_id=1, source_target_pairs={{0,16},{16,0},{32,48},{48,32},{64,80},{80,64},{96,112},{112,96},{1... | collective-permute-start | bytes 20 | tf_op jit(solution)/shard_map/ppermute | solution.py:526
  6.2 5.6 %collective-permute-start.1 = (s32[1,1]{1,0:T(1,128)}, s32[1,1]{1,0:T(1,128)}, u32[]{:S(2)}, u32[]{:S(2)}) collective-permute-start(s32[1,1]{1,0:T(1,128)} %add.3.own), channel_id=1, source_target_pairs={{1,2},{3,4},{5,6},{7,8},{9,10},{11,12},{13,14},{2,1},{4,3},{6,5},{... | collective-permute-start | bytes 20 | tf_op jit(solution)/shard_map/ppermute | solution.py:525
  10.6 1.2 collective-permute-start
  28.2 17.0 %collective-permute-start.4 = (bf16[1024,128]{1,0:T(8,128)(2,1)S(1)}, bf16[1024,128]{1,0:T(8,128)(2,1)S(1)}, u32[]{:S(2)}, u32[]{:S(2)}) collective-permute-start(bf16[1024,128]{1,0:T(8,128)(2,1)S(1)} %get-tuple-element.38), channel_id=1, source_target_pairs={{16,32},{48,64},{80,96},{112,128},{144,160},{176,192},{208,224},{3... | collective-permute-start | bytes 786440 | tf_op jit(solution)/shard_map/ppermute | solution.py:524
  28.9 16.3 %collective-permute-start.5 = (bf16[1024,128]{1,0:T(8,128)(2,1)S(1)}, bf16[1024,128]{1,0:T(8,128)(2,1)S(1)}, u32[]{:S(2)}, u32[]{:S(2)}) collective-permute-start(bf16[1024,128]{1,0:T(8,128)(2,1)S(1)} %get-tuple-element.39), channel_id=1, source_target_pairs={{1,2},{3,4},{5,6},{7,8},{9,10},{11,12},{13,14},{2,1},{4,3},{6,5},{... | collective-permute-start | bytes 786440 | tf_op jit(solution)/shard_map/ppermute | solution.py:525
  32.0 13.2 %collective-permute-start.6 = (bf16[1024,128]{1,0:T(8,128)(2,1)S(1)}, bf16[1024,128]{1,0:T(8,128)(2,1)S(1)}, u32[]{:S(2)}, u32[]{:S(2)}) collective-permute-start(bf16[1024,128]{1,0:T(8,128)(2,1)S(1)} %get-tuple-element.40), channel_id=1, source_target_pairs={{0,16},{16,0},{32,48},{48,32},{64,80},{80,64},{96,112},{112,96},{1... | collective-permute-start | bytes 786440 | tf_op jit(solution)/shard_map/ppermute | solution.py:526
  40.6 4.6 %collective-permute-start.7 = (bf16[1024,128]{1,0:T(8,128)(2,1)S(1)}, bf16[1024,128]{1,0:T(8,128)(2,1)S(1)}, u32[]{:S(2)}, u32[]{:S(2)}) collective-permute-start(bf16[1024,128]{1,0:T(8,128)(2,1)S(1)} %get-tuple-element.41), channel_id=1, source_target_pairs={{0,1},{1,0},{2,3},{3,2},{4,5},{5,4},{6,7},{7,6},{8,9},{9,8},{10,11... | collective-permute-start | bytes 786440 | tf_op jit(solution)/shard_map/ppermute | solution.py:527
  47.7 12.0 %collective-permute-start.8 = (bf16[1024,128]{1,0:T(8,128)(2,1)S(1)}, bf16[1024,128]{1,0:T(8,128)(2,1)S(1)}, u32[]{:S(2)}, u32[]{:S(2)}) collective-permute-start(bf16[1024,128]{1,0:T(8,128)(2,1)S(1)} %get-tuple-element.43), channel_id=1, source_target_pairs={{16,32},{48,64},{80,96},{112,128},{144,160},{176,192},{208,224},{3... | collective-permute-start | bytes 786440 | tf_op jit(solution)/shard_map/ppermute | solution.py:524
  48.4 11.3 %collective-permute-start.9 = (bf16[1024,128]{1,0:T(8,128)(2,1)S(1)}, bf16[1024,128]{1,0:T(8,128)(2,1)S(1)}, u32[]{:S(2)}, u32[]{:S(2)}) collective-permute-start(bf16[1024,128]{1,0:T(8,128)(2,1)S(1)} %get-tuple-element.44), channel_id=1, source_target_pairs={{1,2},{3,4},{5,6},{7,8},{9,10},{11,12},{13,14},{2,1},{4,3},{6,5},{... | collective-permute-start | bytes 786440 | tf_op jit(solution)/shard_map/ppermute | solution.py:525
  52.6 10.1 %collective-permute-start.10 = (bf16[1024,128]{1,0:T(8,128)(2,1)S(1)}, bf16[1024,128]{1,0:T(8,128)(2,1)S(1)}, u32[]{:S(2)}, u32[]{:S(2)}) collective-permute-start(bf16[1024,128]{1,0:T(8,128)(2,1)S(1)} %get-tuple-element.45), channel_id=1, source_target_pairs={{0,16},{16,0},{32,48},{48,32},{64,80},{80,64},{96,112},{112,96},{1... | collective-permute-start | bytes 786440 | tf_op jit(solution)/shard_map/ppermute | solution.py:526
  59.0 3.8 %collective-permute-start.11 = (bf16[1024,128]{1,0:T(8,128)(2,1)S(1)}, bf16[1024,128]{1,0:T(8,128)(2,1)S(1)}, u32[]{:S(2)}, u32[]{:S(2)}) collective-permute-start(bf16[1024,128]{1,0:T(8,128)(2,1)S(1)} %get-tuple-element.46), channel_id=1, source_target_pairs={{0,1},{1,0},{2,3},{3,2},{4,5},{5,4},{6,7},{7,6},{8,9},{9,8},{10,11... | collective-permute-start | bytes 786440 | tf_op jit(solution)/shard_map/ppermute | solution.py:527
  65.3 8.4 %collective-permute-start.12 = (bf16[1024,128]{1,0:T(8,128)(2,1)S(1)}, bf16[1024,128]{1,0:T(8,128)(2,1)S(1)}, u32[]{:S(2)}, u32[]{:S(2)}) collective-permute-start(bf16[1024,128]{1,0:T(8,128)(2,1)S(1)} %get-tuple-element.52), channel_id=1, source_target_pairs={{16,32},{48,64},{80,96},{112,128},{144,160},{176,192},{208,224},{3... | collective-permute-start | bytes 786440 | tf_op jit(solution)/shard_map/ppermute | solution.py:524
  66.0 7.7 %collective-permute-start.13 = (bf16[1024,128]{1,0:T(8,128)(2,1)S(1)}, bf16[1024,128]{1,0:T(8,128)(2,1)S(1)}, u32[]{:S(2)}, u32[]{:S(2)}) collective-permute-start(bf16[1024,128]{1,0:T(8,128)(2,1)S(1)} %get-tuple-element.53), channel_id=1, source_target_pairs={{1,2},{3,4},{5,6},{7,8},{9,10},{11,12},{13,14},{2,1},{4,3},{6,5},{... | collective-permute-start | bytes 786440 | tf_op jit(solution)/shard_map/ppermute | solution.py:525
  69.6 7.1 %collective-permute-start.14 = (bf16[1024,128]{1,0:T(8,128)(2,1)S(1)}, bf16[1024,128]{1,0:T(8,128)(2,1)S(1)}, u32[]{:S(2)}, u32[]{:S(2)}) collective-permute-start(bf16[1024,128]{1,0:T(8,128)(2,1)S(1)} %get-tuple-element.54), channel_id=1, source_target_pairs={{0,16},{16,0},{32,48},{48,32},{64,80},{80,64},{96,112},{112,96},{1... | collective-permute-start | bytes 786440 | tf_op jit(solution)/shard_map/ppermute | solution.py:526
  73.0 3.8 %collective-permute-start.15 = (bf16[1024,128]{1,0:T(8,128)(2,1)S(1)}, bf16[1024,128]{1,0:T(8,128)(2,1)S(1)}, u32[]{:S(2)}, u32[]{:S(2)}) collective-permute-start(bf16[1024,128]{1,0:T(8,128)(2,1)S(1)} %get-tuple-element.55), channel_id=1, source_target_pairs={{0,1},{1,0},{2,3},{3,2},{4,5},{5,4},{6,7},{7,6},{8,9},{9,8},{10,11... | collective-permute-start | bytes 786440 | tf_op jit(solution)/shard_map/ppermute | solution.py:527
where the time goes:
time: 122 us; the launch traced here: 121 us
  starting transfers between devices  41.8 us (34%)
  blocking collectives  39.2 us (32%)
  Pallas kernels  32.6 us (27%)
  waiting for transfers between devices  6.07 us (5%)
  between operations  1.46 us (1%)
    all_to_all x1, blocking collectives, body(): part = lax.all_to_all(part, 'tr', 0, 0, tiled=True)  22.5 us
    ppermute x4, starting transfers between devices, exchange(): lax.ppermute(values[2], 'tr', even_r)  19.1 us
    all_to_all x1, blocking collectives, body(): part = lax.all_to_all(part, 'tc', 0, 0, tiled=True)  16.8 us
    pallas_call x1, Pallas kernels, factor(): pl.pallas_call(factor_kernel, out_shape=[pltpu.VMEM((n, n), F32), square,...  16.4 us
    ppermute x4, starting transfers between devices, exchange(): lax.ppermute(values[1], 'tc', odd_c)  15.4 us
    ppermute x4, waiting for transfers between devices, exchange(): lax.ppermute(values[2], 'tr', even_r)  6.04 us
    pallas_call x2, Pallas kernels, body(): pl.pallas_call(step_kernel, out_shape=[pltpu.VMEM((n, width), F32)] * 2 +...  5.04 us
    ppermute x4, starting transfers between devices, exchange(): lax.ppermute(values[3], 'tc', even_c)  4.16 us
  transfers between devices with their start and end apart: 16, of which 2 were waited for; matrix products, arithmetic and copies ran while one was open for 0% of the time, Pallas kernels for 5%

commit v1 on v0

--- a/solution.py
+++ b/solution.py
@@ -11,6 +11,7 @@
 BASIS = ITERS + 1
 PAIRS = tuple((i, j) for i in range(BASIS) for j in range(i, BASIS))
 LEAF = 256
+ROWS = 256
 SLOTS = 16
 F32 = jnp.float32
 BF16 = jnp.bfloat16
@@ -23,6 +24,10 @@
 
 def smem():
     return pl.BlockSpec(memory_space=pltpu.SMEM)
+
+
+def outside():
+    return pl.BlockSpec(memory_space=pltpu.HBM)
 
 
 def pinned(x, space=pltpu.VMEM):
@@ -90,13 +95,12 @@
     high = inv.astype(BF16)
     resid = eye - (mm(parts[0], high) + mm(parts[1], high))
     yield
-    inv = high.astype(F32) + mm(high, resid.astype(BF16))
+    resid_high = resid.astype(BF16)
+    second = mm(resid_high, resid_high)
     yield
-    inv_parts = split(inv)
-    resid = eye - mm3(parts, inv_parts)
-    yield
-    inv = inv + mm(inv_parts[0], resid.astype(BF16))
-    error = column_norm(resid)
+    more = split(resid + second)
+    inv = high.astype(F32) + (mm(high, more[0]) + mm(high, more[1]))
+    error = column_norm(second)
     return inv * down * across, error
 
 
@@ -234,7 +238,7 @@
     lax.fori_loop(0, blocks - 1, back, 0)
 
 
-def factor_kernel(own, t0, t1, t2, t3, p_hbm, rhs_hbm, c_hbm, d_hbm, work, c_ref, ct_ref, d_ref, rhs_ref, vec, flags, m0, m1, m2, m3, row, times, sems, time_sems):
+def factor_kernel(p_hbm, rhs_hbm, c_hbm, d_hbm, work, c_ref, ct_ref, d_ref, rhs_ref, vec, row, sems):
     n = work.shape[0]
     blocks = n // LEAF
     first = pl.ds(0, LEAF)
@@ -245,13 +249,11 @@
         pltpu.make_async_copy(src, dst, sems.at[len(spots) + i])
         for i, (src, dst) in enumerate(((rhs_hbm, rhs_ref), (c_hbm, c_ref), (d_hbm, d_ref)))
     ]
-    known = [pltpu.make_async_copy(t, times.at[pl.ds(d, 1), :], time_sems.at[d]) for d, t in enumerate((own, t0, t1, t2, t3))]
-
     def before(k):
         if k == 0:
             panels[0].start()
             panels[0].wait()
-            for copy in panels[1:] + others + known:
+            for copy in panels[1:] + others:
                 copy.start()
         elif k == 1:
             others[1].wait()
@@ -276,7 +278,7 @@
 
     worst = eliminate(n, work, vec, extra, before, after)
 
-    @pl.when(jnp.logical_not(jnp.max(worst) < 5e-3))
+    @pl.when(jnp.logical_not(jnp.max(worst) < 4e-3))
     def _():
         for copy in panels:
             copy.start()
@@ -286,34 +288,59 @@
         eliminate_careful(n, work, vec, row)
 
     others[2].wait()
+
+
+def factor(precond, rhs, coupling, diag):
+    n, width = rhs.shape
+    square = pltpu.VMEM((n, n), BF16)
+    column = pltpu.VMEM((n, width), F32)
+    return pl.pallas_call(
+        factor_kernel,
+        out_shape=[pltpu.VMEM((n, n), F32), square, square, square, column, column],
+        in_specs=[outside()] * 4,
+        out_specs=[vmem()] * 6,
+        scratch_shapes=[pltpu.VMEM((LEAF, n), F32), pltpu.SemaphoreType.DMA((n // LEAF + 4,))],
+        compiler_params=params(20),
+    )(*[pinned(x, pltpu.HBM) for x in (precond, rhs, coupling, diag)])
+
+
+def message_kernel(last, own, t1, t2, t3, ct_ref, vec_ref, flags, m0, m1, m2, m3, back, times, sems):
+    known = [pltpu.make_async_copy(t, times.at[pl.ds(d, 1), :], sems.at[d]) for d, t in enumerate((own, t1, t2, t3))]
+    for copy in known:
+        copy.start()
+    high = vec_ref[...].astype(BF16)
+    for k in range(0, back.shape[0], ROWS):
+        rows = pl.ds(k, ROWS)
+        back[rows, :] = mm(ct_ref[rows, :], high).astype(BF16)
     for copy in known:
         copy.wait()
     here = times[0, 0]
-    for d in range(4):
-        flags[0, d] = (times[1 + d, 0] == here + 1).astype(jnp.int32)
-        flags[0, 4 + d] = (times[1 + d, 0] == here - 1).astype(jnp.int32)
-    write_messages(flags, ct_ref, vec, (m0, m1, m2, m3))
-
-
-def factor(tags, precond, rhs, coupling, diag):
-    n, width = rhs.shape
-    square = pltpu.VMEM((n, n), BF16)
-    column = pltpu.VMEM((n, width), F32)
-    outside = pl.BlockSpec(memory_space=pltpu.HBM)
+    next_left = here < last
+    prev_left = here > 1
+    for d in range(1, 4):
+        is_next = times[d, 0] == here + 1
+        is_prev = jnp.logical_and(times[d, 0] == here - 1, here > 1)
+        flags[0, d] = is_next.astype(jnp.int32)
+        flags[0, 4 + d] = is_prev.astype(jnp.int32)
+        next_left = jnp.logical_and(next_left, jnp.logical_not(is_next))
+        prev_left = jnp.logical_and(prev_left, jnp.logical_not(is_prev))
+    flags[0, 0] = next_left.astype(jnp.int32)
+    flags[0, 4] = prev_left.astype(jnp.int32)
+    for k in range(0, back.shape[0], ROWS):
+        rows = pl.ds(k, ROWS)
+        choose_messages(flags, rows, high[k:k + ROWS, :], back[rows, :], (m0, m1, m2, m3))
+
+
+def first_messages(last, tags, flipped, vec):
+    n, width = vec.shape
     return pl.pallas_call(
-        factor_kernel,
-        out_shape=[pltpu.VMEM((n, n), F32), square, square, square, column, column, pltpu.SMEM((1, 8), jnp.int32)]
-        + [jax.ShapeDtypeStruct((n, width), BF16)] * 4,
-        in_specs=[outside] * 9,
-        out_specs=[vmem()] * 6 + [smem()] + [vmem()] * 4,
-        scratch_shapes=[
-            pltpu.VMEM((LEAF, n), F32),
-            pltpu.SMEM((8, 1), jnp.int32),
-            pltpu.SemaphoreType.DMA((n // LEAF + 4,)),
-            pltpu.SemaphoreType.DMA((5,)),
-        ],
-        compiler_params=params(20),
-    )(*[pinned(x, pltpu.HBM) for x in (*tags, precond, rhs, coupling, diag)])
+        functools.partial(message_kernel, last),
+        out_shape=[pltpu.SMEM((1, 8), jnp.int32)] + [jax.ShapeDtypeStruct((n, width), BF16)] * 4,
+        in_specs=[outside()] * 4 + [vmem()] * 2,
+        out_specs=[smem()] + [vmem()] * 4,
+        scratch_shapes=[pltpu.VMEM((n, width), BF16), pltpu.SMEM((8, 1), jnp.int32), pltpu.SemaphoreType.DMA((4,))],
+        compiler_params=params(8),
+    )(*[pinned(t, pltpu.HBM) for t in tags], pinned(flipped), pinned(vec))
 
 
 def build_kernel(work, high_ref, low_ref, size_ref):
@@ -355,8 +382,8 @@
     high, low = split(vec_ref[...])
     both = jnp.concatenate([high, low], axis=1)
     width = high.shape[1]
-    for k in range(0, out_ref.shape[0], LEAF):
-        rows = pl.ds(k, LEAF)
+    for k in range(0, out_ref.shape[0], ROWS):
+        rows = pl.ds(k, ROWS)
         part = mm(high_ref[rows, :], both)
         out_ref[rows, :] = part[:, :width] + (part[:, width:] + mm(low_ref[rows, :], high))
 
@@ -365,22 +392,25 @@
     return [flags[0, d] == 1 for d in range(4)], [flags[0, 4 + d] == 1 for d in range(4)]
 
 
+def choose_messages(flags, rows, ahead, back, out_refs):
+    is_next, is_prev = relation(flags)
+    for d, out in enumerate(out_refs):
+        out[rows, :] = jnp.where(is_next[d], ahead, jnp.where(is_prev[d], back, jnp.zeros_like(back)))
+
+
 def write_messages(flags, ct_ref, vec_ref, out_refs):
-    is_next, is_prev = relation(flags)
     high = vec_ref[...].astype(BF16)
-    for k in range(0, vec_ref.shape[0], LEAF):
-        rows = pl.ds(k, LEAF)
+    for k in range(0, vec_ref.shape[0], ROWS):
+        rows = pl.ds(k, ROWS)
         back = mm(ct_ref[rows, :], high).astype(BF16)
-        ahead = high[k:k + LEAF, :]
-        for d, out in enumerate(out_refs):
-            out[rows, :] = jnp.where(is_next[d], ahead, jnp.where(is_prev[d], back, jnp.zeros_like(back)))
+        choose_messages(flags, rows, high[k:k + ROWS, :], back, out_refs)
 
 
 def own_kernel(diag_ref, vec_ref, out_ref):
     both = jnp.concatenate(split(vec_ref[...]), axis=1)
     width = vec_ref.shape[1]
-    for k in range(0, out_ref.shape[0], LEAF):
-        rows = pl.ds(k, LEAF)
+    for k in range(0, out_ref.shape[0], ROWS):
+        rows = pl.ds(k, ROWS)
         part = mm(diag_ref[rows, :], both)
         out_ref[rows, :] = part[:, :width] + part[:, width:]
 
@@ -391,9 +421,9 @@
     before = zero
     for d, ref in enumerate(got):
         before = jnp.where(is_prev[d], ref[...], before)
-    for k in range(0, out_ref.shape[0], LEAF):
-        rows = pl.ds(k, LEAF)
-        after = zero[:LEAF]
+    for k in range(0, out_ref.shape[0], ROWS):
+        rows = pl.ds(k, ROWS)
+        after = zero[:ROWS]
         for d, ref in enumerate(got):
             after = jnp.where(is_next[d], ref[rows, :], after)
         out_ref[rows, :] = own_ref[rows, :] + mm(c_ref[rows, :], before) + after.astype(F32)
@@ -520,23 +550,19 @@
 def exchange(values):
     even_r, odd_r = neighbour_perms(lax.axis_size("tr"))
     even_c, odd_c = neighbour_perms(lax.axis_size("tc"))
-    return [
-        lax.ppermute(values[0], "tr", odd_r),
-        lax.ppermute(values[1], "tc", odd_c),
-        lax.ppermute(values[2], "tr", even_r),
-        lax.ppermute(values[3], "tc", even_c),
-    ]
+    routes = (("tr", odd_r), ("tc", odd_c), ("tr", even_r), ("tc", even_c))
+    return [None if v is None else lax.ppermute(v, *route) for v, route in zip(values, routes)]
 
 
 def body(diag_block, coupling, precond, rhs, slot_time):
     n, width = rhs.shape[2:]
     own_tag = slot_time + 1
-    tags = [own_tag] + exchange([own_tag] * 4)
+    tags = [own_tag] + exchange([None] + [own_tag] * 3)[1:]
+    last = lax.axis_size("tr") * lax.axis_size("tc")
     sent = [jax.ShapeDtypeStruct((n, width), BF16)] * 4
 
-    work, c_here, flipped, diag_here, res, vec, flags, *messages = factor(
-        tags, precond[0, 0], rhs[0, 0], coupling[0, 0], diag_block[0, 0]
-    )
+    work, c_here, flipped, diag_here, res, vec = factor(precond[0, 0], rhs[0, 0], coupling[0, 0], diag_block[0, 0])
+    flags, *messages = first_messages(last, tags, flipped, vec)
     basis = [res, vec]
     for step in range(ITERS):
         got = exchange(messages)
@@ -562,7 +588,7 @@
             messages = out[2:]
     part = pl.pallas_call(
         last_kernel,
-        out_shape=jax.ShapeDtypeStruct((lax.axis_size("tc") * SLOTS, width), F32),
+        out_shape=pltpu.VMEM((lax.axis_size("tc") * SLOTS, width), F32),
         in_specs=[smem()] + [vmem()] * 15,
         out_specs=vmem(),
         scratch_shapes=[pltpu.VMEM((n, width), F32)] * 2,
@@ -571,10 +597,10 @@
     part = lax.all_to_all(part, "tc", 0, 0, tiled=True)
     part = pl.pallas_call(
         merge_kernel,
-        out_shape=jax.ShapeDtypeStruct((lax.axis_size("tr") * SLOTS, width), F32),
+        out_shape=pltpu.VMEM((lax.axis_size("tr") * SLOTS, width), F32),
         in_specs=[vmem()],
         out_specs=vmem(),
-    )(part)
+    )(pinned(part))
     part = lax.all_to_all(part, "tr", 0, 0, tiled=True)
     solution, norm = pl.pallas_call(
         finish_kernel,
@@ -582,7 +608,7 @@
         in_specs=[vmem()] * 4,
         out_specs=[vmem()] * 2,
         compiler_params=params(8),
-    )(part, pinned(basis[1]), pinned(basis[3]), pinned(basis[5]))
+    )(pinned(part), pinned(basis[1]), pinned(basis[3]), pinned(basis[5]))
     return (solution[None, None], norm[0])
 
 

time: 122 us -> 113 us (0.926)
  waiting for transfers between devices: 6.07 us -> 21.3 us
  starting transfers between devices: 41.8 us -> 28.6 us
  blocking collectives: 39.2 us -> 30.7 us
  Pallas kernels: 32.6 us -> 30.3 us
    ppermute x16 -> x15, waiting for transfers between devices: 6.07 us -> 21.3 us  [exchange(): lax.ppermute(v, *route)]
    ppermute x16 -> x15, starting transfers between devices: 41.8 us -> 28.6 us  [exchange(): lax.ppermute(v, *route)]
    all_to_all x1, blocking collectives: 22.5 us -> 16.4 us  [body(): part = lax.all_to_all(part, 'tr', 0, 0, tiled=True)]
    pallas_call x1, Pallas kernels: 16.4 us -> 12.5 us  [factor(): pl.pallas_call(factor_kernel, out_shape=[pltpu.VMEM((n, n), F32), square,...]
    all_to_all x1, blocking collectives: 16.8 us -> 14.3 us  [body(): part = lax.all_to_all(part, 'tc', 0, 0, tiled=True)]
    pallas_call x2 -> x3, Pallas kernels: 4.1 us -> 5.78 us  [the longest x1 3.27 us: first_messages(): pl.pallas_call(functools.partial(message_kernel, last), out_shape=[pltpu....]
  transfers between devices with their start and end apart: 16 -> 15, of which waited for: 2 -> 3; matrix products, arithmetic and copies ran while one was open for 0% -> 0% of each run, Pallas kernels for 5% -> 16%
where the time goes in v1:
time: 113 us; the launch traced here: 112 us
  blocking collectives  30.7 us (27%)
  Pallas kernels  30.3 us (27%)
  starting transfers between devices  28.6 us (25%)
  waiting for transfers between devices  21.3 us (19%)
  between operations  1.45 us (1%)
    ppermute x15, starting transfers between devices, exchange(): lax.ppermute(v, *route)  28.6 us
    ppermute x15, waiting for transfers between devices, exchange(): lax.ppermute(v, *route)  21.3 us
    all_to_all x1, blocking collectives, body(): part = lax.all_to_all(part, 'tr', 0, 0, tiled=True)  16.4 us
    all_to_all x1, blocking collectives, body(): part = lax.all_to_all(part, 'tc', 0, 0, tiled=True)  14.3 us
    pallas_call x1, Pallas kernels, factor(): pl.pallas_call(factor_kernel, out_shape=[pltpu.VMEM((n, n), F32), square,...  12.5 us
    pallas_call x2, Pallas kernels, body(): pl.pallas_call(step_kernel, out_shape=[pltpu.VMEM((n, width), F32)] * 2 +...  5.01 us
    pallas_call x1, Pallas kernels, build(): pl.pallas_call(build_kernel, out_shape=[pltpu.VMEM((n, n), BF16), pltpu.V...  3.8 us
    pallas_call x1, Pallas kernels, first_messages(): pl.pallas_call(functools.partial(message_kernel, last), out_shape=[pltpu....  3.27 us
  transfers between devices with their start and end apart: 15, of which 3 were waited for; matrix products, arithmetic and copies ran while one was open for 0% of the time, Pallas kernels for 16%

profile of v1, /device:TPU:1, one launch (start us, length us, event | category | flops | bytes accessed | tf_op | source)
XLA Modules:
  0.0 112.2 jit_solution(2669651594612972119)
XLA Ops:
  1.3 4.1 %collective-permute-start.2 = (s32[1,1]{1,0:T(1,128)}, s32[1,1]{1,0:T(1,128)}, u32[]{:S(2)}, u32[]{:S(2)}) collective-permute-start(s32[1,1]{1,0:T(1,128)} %add.3.own), channel_id=1, source_target_pairs={{0,1},{1,0},{2,3},{3,2},{4,5},{5,4},{6,7},{7,6},{8,9},{9,8},{10,11... | collective-permute-start | bytes 20 | tf_op jit(solution)/shard_map/ppermute | solution.py:554
  5.4 0.7 collective-permute-start.1
  6.2 4.5 %collective-permute-start = (s32[1,1]{1,0:T(1,128)}, s32[1,1]{1,0:T(1,128)}, u32[]{:S(2)}, u32[]{:S(2)}) collective-permute-start(s32[1,1]{1,0:T(1,128)} %add.3.own), channel_id=1, source_target_pairs={{1,2},{3,4},{5,6},{7,8},{9,10},{11,12},{13,14},{2,1},{4,3},{6,5},{... | collective-permute-start | bytes 20 | tf_op jit(solution)/shard_map/ppermute | solution.py:554
  10.6 12.5 %shard_map.68 = (f32[1024,1024]{1,0:T(8,128)S(1)}, bf16[1024,1024]{1,0:T(8,128)(2,1)S(1)}, bf16[1024,1024]{1,0:T(8,128)(2,1)S(1)}, bf16[1024,1024]{1,0:T(8,128)(...) custom-call(f32[1024,1024]{1,0:T(8,128)} %bitcast.14, f32[1024,128]{1,0:T(8,128)} %bitcast.17, ...), custom_call_target="tpu_custom_call" | custom-call | tf_op jit(solution)/shard_map/pallas_call | solution.py:297
  23.1 3.3 %shard_map.69 = (s32[1,8]{1,0:T(1,128)S(4)}, bf16[1024,128]{1,0:T(8,128)(2,1)S(1)}, bf16[1024,128]{1,0:T(8,128)(2,1)S(1)}, bf16[1024,128]{1,0:T(8,128)(2,1)S(1)}, bf16[1024,128]{1,0:T(8,128)(2,1)S(1)}) custom-call(s32[1,1]{1,0:T(1,128)} %add.3.own, s32[1,1]{1,0:T(1,128)} %collective-permute-done.t1, s32[1,1]{1,0:T(1,128)} %collective-permute-done.1.t2, ...), custom_call_target="tpu_custom_call" | custom-call | tf_op jit(solution)/shard_map/pallas_call | solution.py:336
  26.4 0.7 collective-permute-start.3
  27.1 2.5 %collective-permute-start.4 = (bf16[1024,128]{1,0:T(8,128)(2,1)S(1)}, bf16[1024,128]{1,0:T(8,128)(2,1)S(1)}, u32[]{:S(2)}, u32[]{:S(2)}) collective-permute-start(bf16[1024,128]{1,0:T(8,128)(2,1)S(1)} %get-tuple-element.39), channel_id=1, source_target_pairs={{1,2},{3,4},{5,6},{7,8},{9,10},{11,12},{13,14},{2,1},{4,3},{6,5},{... | collective-permute-start | bytes 786440 | tf_op jit(solution)/shard_map/ppermute | solution.py:554
  29.6 4.9 %collective-permute-start.5 = (bf16[1024,128]{1,0:T(8,128)(2,1)S(1)}, bf16[1024,128]{1,0:T(8,128)(2,1)S(1)}, u32[]{:S(2)}, u32[]{:S(2)}) collective-permute-start(bf16[1024,128]{1,0:T(8,128)(2,1)S(1)} %get-tuple-element.40), channel_id=1, source_target_pairs={{0,16},{16,0},{32,48},{48,32},{64,80},{80,64},{96,112},{112,96},{1... | collective-permute-start | bytes 786440 | tf_op jit(solution)/shard_map/ppermute | solution.py:554
  34.5 0.0 collective-permute-start.6
  34.5 3.8 %shard_map.71 = (bf16[1024,1024]{1,0:T(8,128)(2,1)S(1)}, bf16[1024,1024]{1,0:T(8,128)(2,1)S(1)}, f32[8,128]{1,0:T(8,128)S(1)}) custom-call(f32[1024,1024]{1,0:T(8,128)S(1)} %get-tuple-element.35.work), custom_call_target="tpu_custom_call" | custom-call | tf_op jit(solution)/shard_map/pallas_call | solution.py:372
  38.3 0.7 shard_map.70.own_ref
  39.0 3.8 %collective-permute-done.4.g1 = bf16[1024,128]{1,0:T(8,128)(2,1)S(1)} collective-permute-done((bf16[1024,128]{1,0:T(8,128)(2,1)S(1)}, bf16[1024,128]{1,0:T(8,128)(2,1)S(1)}, u32[]{:S(2)}, u32[]{:S(2)}) %collective-permute-start.4) | collective-permute-done | bytes 262176 | tf_op jit(solution)/shard_map/ppermute | solution.py:554
  42.9 2.5 %shard_map.72 = (f32[1024,128]{1,0:T(8,128)S(1)}, f32[1024,128]{1,0:T(8,128)S(1)}, bf16[1024,128]{1,0:T(8,128)(2,1)S(1)}, bf16[1024,128]{1,0:T(8,128)(2,1)S(1)},...) custom-call(s32[1,8]{1,0:T(1,128)S(4)} %get-tuple-element.32.flags, f32[1024,128]{1,0:T(8,128)S(1)} %shard_map.70.own_ref, ...), custom_call_target="tpu_custom_call" | custom-call | tf_op jit(solution)/shard_map/pallas_call | solution.py:579
  45.4 0.7 collective-permute-start.7
  46.1 1.9 %collective-permute-start.8 = (bf16[1024,128]{1,0:T(8,128)(2,1)S(1)}, bf16[1024,128]{1,0:T(8,128)(2,1)S(1)}, u32[]{:S(2)}, u32[]{:S(2)}) collective-permute-start(bf16[1024,128]{1,0:T(8,128)(2,1)S(1)} %get-tuple-element.44), channel_id=1, source_target_pairs={{1,2},{3,4},{5,6},{7,8},{9,10},{11,12},{13,14},{2,1},{4,3},{6,5},{... | collective-permute-start | bytes 786440 | tf_op jit(solution)/shard_map/ppermute | solution.py:554
  48.0 4.4 %collective-permute-start.9 = (bf16[1024,128]{1,0:T(8,128)(2,1)S(1)}, bf16[1024,128]{1,0:T(8,128)(2,1)S(1)}, u32[]{:S(2)}, u32[]{:S(2)}) collective-permute-start(bf16[1024,128]{1,0:T(8,128)(2,1)S(1)} %get-tuple-element.45), channel_id=1, source_target_pairs={{0,16},{16,0},{32,48},{48,32},{64,80},{80,64},{96,112},{112,96},{1... | collective-permute-start | bytes 786440 | tf_op jit(solution)/shard_map/ppermute | solution.py:554
  52.4 0.0 collective-permute-start.10
  52.4 0.7 shard_map.73.own_ref
  53.2 7.7 %collective-permute-done.8.g1 = bf16[1024,128]{1,0:T(8,128)(2,1)S(1)} collective-permute-done((bf16[1024,128]{1,0:T(8,128)(2,1)S(1)}, bf16[1024,128]{1,0:T(8,128)(2,1)S(1)}, u32[]{:S(2)}, u32[]{:S(2)}) %collective-permute-start.8) | collective-permute-done | bytes 262176 | tf_op jit(solution)/shard_map/ppermute | solution.py:554
  60.9 0.0 collective-permute-done.9.g2
  60.9 0.0 collective-permute-done.10.g3
  60.9 2.5 %shard_map.74 = (f32[1024,128]{1,0:T(8,128)S(1)}, f32[1024,128]{1,0:T(8,128)S(1)}, bf16[1024,128]{1,0:T(8,128)(2,1)S(1)}, bf16[1024,128]{1,0:T(8,128)(2,1)S(1)},...) custom-call(s32[1,8]{1,0:T(1,128)S(4)} %get-tuple-element.32.flags, f32[1024,128]{1,0:T(8,128)S(1)} %shard_map.73.own_ref, ...), custom_call_target="tpu_custom_call" | custom-call | tf_op jit(solution)/shard_map/pallas_call | solution.py:579
  63.4 0.7 collective-permute-start.11
  64.1 1.9 %collective-permute-start.12 = (bf16[1024,128]{1,0:T(8,128)(2,1)S(1)}, bf16[1024,128]{1,0:T(8,128)(2,1)S(1)}, u32[]{:S(2)}, u32[]{:S(2)}) collective-permute-start(bf16[1024,128]{1,0:T(8,128)(2,1)S(1)} %get-tuple-element.53), channel_id=1, source_target_pairs={{1,2},{3,4},{5,6},{7,8},{9,10},{11,12},{13,14},{2,1},{4,3},{6,5},{... | collective-permute-start | bytes 786440 | tf_op jit(solution)/shard_map/ppermute | solution.py:554
  66.0 1.5 %collective-permute-start.13 = (bf16[1024,128]{1,0:T(8,128)(2,1)S(1)}, bf16[1024,128]{1,0:T(8,128)(2,1)S(1)}, u32[]{:S(2)}, u32[]{:S(2)}) collective-permute-start(bf16[1024,128]{1,0:T(8,128)(2,1)S(1)} %get-tuple-element.54), channel_id=1, source_target_pairs={{0,16},{16,0},{32,48},{48,32},{64,80},{80,64},{96,112},{112,96},{1... | collective-permute-start | bytes 786440 | tf_op jit(solution)/shard_map/ppermute | solution.py:554
  67.6 0.7 shard_map.75.own_ref
  68.3 9.7 %collective-permute-done.12.g1 = bf16[1024,128]{1,0:T(8,128)(2,1)S(1)} collective-permute-done((bf16[1024,128]{1,0:T(8,128)(2,1)S(1)}, bf16[1024,128]{1,0:T(8,128)(2,1)S(1)}, u32[]{:S(2)}, u32[]{:S(2)}) %collective-permute-start.12) | collective-permute-done | bytes 262176 | tf_op jit(solution)/shard_map/ppermute | solution.py:554
  78.0 2.4 %shard_map.76 = f32[256,128]{1,0:T(8,128)S(1)} custom-call(s32[1,8]{1,0:T(1,128)S(4)} %get-tuple-element.32.flags, f32[1024,128]{1,0:T(8,128)S(1)} %shard_map.75.own_ref, bf16[1024,1024]{1,0:T(8,128)(2,1)S(1)} %get-tuple-element.34.c_ref, bf16[1024,1024]{1,0:T(8,128)(2,1)S(1)} %get-tuple-element.36.high_ref, ...), custom_call_target="tpu_custom_call" | custom-call | tf_op jit(solution)/shard_map/pallas_call | solution.py:589
  80.4 14.3 %all_to_all.22 = f32[16,16,128]{2,1,0:T(8,128)S(1)} all-to-all(f32[16,16,128]{2,1,0:T(8,128)S(1)} %bitcast.13), channel_id=1, replica_groups=mesh['tr'=16,'tc'=16] {'tc'}, dimensions={0} | all-to-all | bytes 262144 | tf_op jit(solution)/shard_map/all_to_all | solution.py:597
  94.7 0.1 shard_map.77
  94.8 16.4 %all_to_all.23 = f32[16,16,128]{2,1,0:T(8,128)S(1)} all-to-all(f32[16,16,128]{2,1,0:T(8,128)S(1)} %bitcast.11), channel_id=1, replica_groups=mesh['tr'=16,'tc'=16] {'tr'}, dimensions={0} | all-to-all | bytes 262144 | tf_op jit(solution)/shard_map/all_to_all | solution.py:604
  111.2 1.1 shard_map.78
  (11 shorter events, 0.0 us)
Async XLA Ops:
  1.3 21.8 %collective-permute-start.2 = (s32[1,1]{1,0:T(1,128)}, s32[1,1]{1,0:T(1,128)}, u32[]{:S(2)}, u32[]{:S(2)}) collective-permute-start(s32[1,1]{1,0:T(1,128)} %add.3.own), channel_id=1, source_target_pairs={{0,1},{1,0},{2,3},{3,2},{4,5},{5,4},{6,7},{7,6},{8,9},{9,8},{10,11... | collective-permute-start | bytes 20 | tf_op jit(solution)/shard_map/ppermute | solution.py:554
  5.4 17.7 %collective-permute-start.1 = (s32[1,1]{1,0:T(1,128)}, s32[1,1]{1,0:T(1,128)}, u32[]{:S(2)}, u32[]{:S(2)}) collective-permute-start(s32[1,1]{1,0:T(1,128)} %add.3.own), channel_id=1, source_target_pairs={{0,16},{16,0},{32,48},{48,32},{64,80},{80,64},{96,112},{112,96},{1... | collective-permute-start | bytes 20 | tf_op jit(solution)/shard_map/ppermute | solution.py:554
  6.2 17.0 %collective-permute-start = (s32[1,1]{1,0:T(1,128)}, s32[1,1]{1,0:T(1,128)}, u32[]{:S(2)}, u32[]{:S(2)}) collective-permute-start(s32[1,1]{1,0:T(1,128)} %add.3.own), channel_id=1, source_target_pairs={{1,2},{3,4},{5,6},{7,8},{9,10},{11,12},{13,14},{2,1},{4,3},{6,5},{... | collective-permute-start | bytes 20 | tf_op jit(solution)/shard_map/ppermute | solution.py:554
  26.4 12.6 %collective-permute-start.3 = (bf16[1024,128]{1,0:T(8,128)(2,1)S(1)}, bf16[1024,128]{1,0:T(8,128)(2,1)S(1)}, u32[]{:S(2)}, u32[]{:S(2)}) collective-permute-start(bf16[1024,128]{1,0:T(8,128)(2,1)S(1)} %get-tuple-element.38), channel_id=1, source_target_pairs={{16,32},{48,64},{80,96},{112,128},{144,160},{176,192},{208,224},{3... | collective-permute-start | bytes 786440 | tf_op jit(solution)/shard_map/ppermute | solution.py:554
  27.1 15.8 %collective-permute-start.4 = (bf16[1024,128]{1,0:T(8,128)(2,1)S(1)}, bf16[1024,128]{1,0:T(8,128)(2,1)S(1)}, u32[]{:S(2)}, u32[]{:S(2)}) collective-permute-start(bf16[1024,128]{1,0:T(8,128)(2,1)S(1)} %get-tuple-element.39), channel_id=1, source_target_pairs={{1,2},{3,4},{5,6},{7,8},{9,10},{11,12},{13,14},{2,1},{4,3},{6,5},{... | collective-permute-start | bytes 786440 | tf_op jit(solution)/shard_map/ppermute | solution.py:554
  29.6 13.3 %collective-permute-start.5 = (bf16[1024,128]{1,0:T(8,128)(2,1)S(1)}, bf16[1024,128]{1,0:T(8,128)(2,1)S(1)}, u32[]{:S(2)}, u32[]{:S(2)}) collective-permute-start(bf16[1024,128]{1,0:T(8,128)(2,1)S(1)} %get-tuple-element.40), channel_id=1, source_target_pairs={{0,16},{16,0},{32,48},{48,32},{64,80},{80,64},{96,112},{112,96},{1... | collective-permute-start | bytes 786440 | tf_op jit(solution)/shard_map/ppermute | solution.py:554
  34.5 8.4 %collective-permute-start.6 = (bf16[1024,128]{1,0:T(8,128)(2,1)S(1)}, bf16[1024,128]{1,0:T(8,128)(2,1)S(1)}, u32[]{:S(2)}, u32[]{:S(2)}) collective-permute-start(bf16[1024,128]{1,0:T(8,128)(2,1)S(1)} %get-tuple-element.41), channel_id=1, source_target_pairs={{0,1},{1,0},{2,3},{3,2},{4,5},{5,4},{6,7},{7,6},{8,9},{9,8},{10,11... | collective-permute-start | bytes 786440 | tf_op jit(solution)/shard_map/ppermute | solution.py:554
  45.4 7.8 %collective-permute-start.7 = (bf16[1024,128]{1,0:T(8,128)(2,1)S(1)}, bf16[1024,128]{1,0:T(8,128)(2,1)S(1)}, u32[]{:S(2)}, u32[]{:S(2)}) collective-permute-start(bf16[1024,128]{1,0:T(8,128)(2,1)S(1)} %get-tuple-element.43), channel_id=1, source_target_pairs={{16,32},{48,64},{80,96},{112,128},{144,160},{176,192},{208,224},{3... | collective-permute-start | bytes 786440 | tf_op jit(solution)/shard_map/ppermute | solution.py:554
  46.1 14.8 %collective-permute-start.8 = (bf16[1024,128]{1,0:T(8,128)(2,1)S(1)}, bf16[1024,128]{1,0:T(8,128)(2,1)S(1)}, u32[]{:S(2)}, u32[]{:S(2)}) collective-permute-start(bf16[1024,128]{1,0:T(8,128)(2,1)S(1)} %get-tuple-element.44), channel_id=1, source_target_pairs={{1,2},{3,4},{5,6},{7,8},{9,10},{11,12},{13,14},{2,1},{4,3},{6,5},{... | collective-permute-start | bytes 786440 | tf_op jit(solution)/shard_map/ppermute | solution.py:554
  48.0 12.9 %collective-permute-start.9 = (bf16[1024,128]{1,0:T(8,128)(2,1)S(1)}, bf16[1024,128]{1,0:T(8,128)(2,1)S(1)}, u32[]{:S(2)}, u32[]{:S(2)}) collective-permute-start(bf16[1024,128]{1,0:T(8,128)(2,1)S(1)} %get-tuple-element.45), channel_id=1, source_target_pairs={{0,16},{16,0},{32,48},{48,32},{64,80},{80,64},{96,112},{112,96},{1... | collective-permute-start | bytes 786440 | tf_op jit(solution)/shard_map/ppermute | solution.py:554
  52.4 8.5 %collective-permute-start.10 = (bf16[1024,128]{1,0:T(8,128)(2,1)S(1)}, bf16[1024,128]{1,0:T(8,128)(2,1)S(1)}, u32[]{:S(2)}, u32[]{:S(2)}) collective-permute-start(bf16[1024,128]{1,0:T(8,128)(2,1)S(1)} %get-tuple-element.46), channel_id=1, source_target_pairs={{0,1},{1,0},{2,3},{3,2},{4,5},{5,4},{6,7},{7,6},{8,9},{9,8},{10,11... | collective-permute-start | bytes 786440 | tf_op jit(solution)/shard_map/ppermute | solution.py:554
  63.4 4.9 %collective-permute-start.11 = (bf16[1024,128]{1,0:T(8,128)(2,1)S(1)}, bf16[1024,128]{1,0:T(8,128)(2,1)S(1)}, u32[]{:S(2)}, u32[]{:S(2)}) collective-permute-start(bf16[1024,128]{1,0:T(8,128)(2,1)S(1)} %get-tuple-element.52), channel_id=1, source_target_pairs={{16,32},{48,64},{80,96},{112,128},{144,160},{176,192},{208,224},{3... | collective-permute-start | bytes 786440 | tf_op jit(solution)/shard_map/ppermute | solution.py:554
  64.1 13.9 %collective-permute-start.12 = (bf16[1024,128]{1,0:T(8,128)(2,1)S(1)}, bf16[1024,128]{1,0:T(8,128)(2,1)S(1)}, u32[]{:S(2)}, u32[]{:S(2)}) collective-permute-start(bf16[1024,128]{1,0:T(8,128)(2,1)S(1)} %get-tuple-element.53), channel_id=1, source_target_pairs={{1,2},{3,4},{5,6},{7,8},{9,10},{11,12},{13,14},{2,1},{4,3},{6,5},{... | collective-permute-start | bytes 786440 | tf_op jit(solution)/shard_map/ppermute | solution.py:554
  66.0 11.9 %collective-permute-start.13 = (bf16[1024,128]{1,0:T(8,128)(2,1)S(1)}, bf16[1024,128]{1,0:T(8,128)(2,1)S(1)}, u32[]{:S(2)}, u32[]{:S(2)}) collective-permute-start(bf16[1024,128]{1,0:T(8,128)(2,1)S(1)} %get-tuple-element.54), channel_id=1, source_target_pairs={{0,16},{16,0},{32,48},{48,32},{64,80},{80,64},{96,112},{112,96},{1... | collective-permute-start | bytes 786440 | tf_op jit(solution)/shard_map/ppermute | solution.py:554
  67.6 10.4 %collective-permute-start.14 = (bf16[1024,128]{1,0:T(8,128)(2,1)S(1)}, bf16[1024,128]{1,0:T(8,128)(2,1)S(1)}, u32[]{:S(2)}, u32[]{:S(2)}) collective-permute-start(bf16[1024,128]{1,0:T(8,128)(2,1)S(1)} %get-tuple-element.55), channel_id=1, source_target_pairs={{0,1},{1,0},{2,3},{3,2},{4,5},{5,4},{6,7},{7,6},{8,9},{9,8},{10,11... | collective-permute-start | bytes 786440 | tf_op jit(solution)/shard_map/ppermute | solution.py:554

commit v2 on v1

--- a/solution.py
+++ b/solution.py
@@ -238,7 +238,7 @@
     lax.fori_loop(0, blocks - 1, back, 0)
 
 
-def factor_kernel(p_hbm, rhs_hbm, c_hbm, d_hbm, work, c_ref, ct_ref, d_ref, rhs_ref, vec, row, sems):
+def factor_kernel(time, p_hbm, rhs_hbm, c_hbm, d_hbm, work, c_ref, ct_ref, d_ref, rhs_ref, vec, tag, row, sems):
     n = work.shape[0]
     blocks = n // LEAF
     first = pl.ds(0, LEAF)
@@ -288,38 +288,38 @@
         eliminate_careful(n, work, vec, row)
 
     others[2].wait()
-
-
-def factor(precond, rhs, coupling, diag):
+    tag[...] = jnp.full(tag.shape, time[0, 0] + 1, jnp.int32)
+
+
+def factor(precond, rhs, coupling, diag, time):
     n, width = rhs.shape
     square = pltpu.VMEM((n, n), BF16)
     column = pltpu.VMEM((n, width), F32)
     return pl.pallas_call(
         factor_kernel,
-        out_shape=[pltpu.VMEM((n, n), F32), square, square, square, column, column],
-        in_specs=[outside()] * 4,
-        out_specs=[vmem()] * 6,
+        out_shape=[pltpu.VMEM((n, n), F32), square, square, square, column, column, jax.ShapeDtypeStruct(time.shape, jnp.int32)],
+        in_specs=[smem()] + [outside()] * 4,
+        out_specs=[vmem()] * 7,
         scratch_shapes=[pltpu.VMEM((LEAF, n), F32), pltpu.SemaphoreType.DMA((n // LEAF + 4,))],
         compiler_params=params(20),
-    )(*[pinned(x, pltpu.HBM) for x in (precond, rhs, coupling, diag)])
-
-
-def message_kernel(last, own, t1, t2, t3, ct_ref, vec_ref, flags, m0, m1, m2, m3, back, times, sems):
-    known = [pltpu.make_async_copy(t, times.at[pl.ds(d, 1), :], sems.at[d]) for d, t in enumerate((own, t1, t2, t3))]
-    for copy in known:
-        copy.start()
+    )(time, *[pinned(x, pltpu.HBM) for x in (precond, rhs, coupling, diag)])
+
+
+def back_kernel(ct_ref, vec_ref, ahead, back):
     high = vec_ref[...].astype(BF16)
+    ahead[...] = high
     for k in range(0, back.shape[0], ROWS):
         rows = pl.ds(k, ROWS)
         back[rows, :] = mm(ct_ref[rows, :], high).astype(BF16)
-    for copy in known:
-        copy.wait()
-    here = times[0, 0]
+
+
+def message_kernel(last, own, t1, t2, t3, ahead, back, flags, m0, m1, m2, m3):
+    here, *times = [jnp.max(t[...]) for t in (own, t1, t2, t3)]
     next_left = here < last
     prev_left = here > 1
-    for d in range(1, 4):
-        is_next = times[d, 0] == here + 1
-        is_prev = jnp.logical_and(times[d, 0] == here - 1, here > 1)
+    for d, time in enumerate(times, 1):
+        is_next = time == here + 1
+        is_prev = jnp.logical_and(time == here - 1, here > 1)
         flags[0, d] = is_next.astype(jnp.int32)
         flags[0, 4 + d] = is_prev.astype(jnp.int32)
         next_left = jnp.logical_and(next_left, jnp.logical_not(is_next))
@@ -328,19 +328,25 @@
     flags[0, 4] = prev_left.astype(jnp.int32)
     for k in range(0, back.shape[0], ROWS):
         rows = pl.ds(k, ROWS)
-        choose_messages(flags, rows, high[k:k + ROWS, :], back[rows, :], (m0, m1, m2, m3))
+        choose_messages(flags, rows, ahead[rows, :], back[rows, :], (m0, m1, m2, m3))
 
 
 def first_messages(last, tags, flipped, vec):
     n, width = vec.shape
+    parts = pl.pallas_call(
+        back_kernel,
+        out_shape=[pltpu.VMEM((n, width), BF16)] * 2,
+        in_specs=[vmem()] * 2,
+        out_specs=[vmem()] * 2,
+        compiler_params=params(8),
+    )(pinned(flipped), pinned(vec))
     return pl.pallas_call(
         functools.partial(message_kernel, last),
         out_shape=[pltpu.SMEM((1, 8), jnp.int32)] + [jax.ShapeDtypeStruct((n, width), BF16)] * 4,
-        in_specs=[outside()] * 4 + [vmem()] * 2,
+        in_specs=[vmem()] * 6,
         out_specs=[smem()] + [vmem()] * 4,
-        scratch_shapes=[pltpu.VMEM((n, width), BF16), pltpu.SMEM((8, 1), jnp.int32), pltpu.SemaphoreType.DMA((4,))],
         compiler_params=params(8),
-    )(*[pinned(t, pltpu.HBM) for t in tags], pinned(flipped), pinned(vec))
+    )(*[pinned(t) for t in tags], *[pinned(p) for p in parts])
 
 
 def build_kernel(work, high_ref, low_ref, size_ref):
@@ -554,14 +560,27 @@
     return [None if v is None else lax.ppermute(v, *route) for v, route in zip(values, routes)]
 
 
+def reduce_groups():
+    rows, cols = lax.axis_size("tr"), lax.axis_size("tc")
+    deep = rows // 2
+
+    def rank(h, z, q, c):
+        return (h * deep + z) * cols + q * 2 + c
+
+    lines = [[rank(h, z, q, c) for z in range(deep) for c in range(2)] for h in range(2) for q in range(cols // 2)]
+    planes = [[rank(h, z, q, c) for h in range(2) for q in range(cols // 2)] for z in range(deep) for c in range(2)]
+    return lines, planes
+
+
 def body(diag_block, coupling, precond, rhs, slot_time):
     n, width = rhs.shape[2:]
-    own_tag = slot_time + 1
-    tags = [own_tag] + exchange([None] + [own_tag] * 3)[1:]
     last = lax.axis_size("tr") * lax.axis_size("tc")
     sent = [jax.ShapeDtypeStruct((n, width), BF16)] * 4
 
-    work, c_here, flipped, diag_here, res, vec = factor(precond[0, 0], rhs[0, 0], coupling[0, 0], diag_block[0, 0])
+    work, c_here, flipped, diag_here, res, vec, own_tag = factor(
+        precond[0, 0], rhs[0, 0], coupling[0, 0], diag_block[0, 0], slot_time
+    )
+    tags = [own_tag] + exchange([None] + [own_tag] * 3)[1:]
     flags, *messages = first_messages(last, tags, flipped, vec)
     basis = [res, vec]
     for step in range(ITERS):
@@ -586,22 +605,23 @@
             vec = out[1]
             basis += [out[0], vec]
             messages = out[2:]
+    lines, planes = reduce_groups()
     part = pl.pallas_call(
         last_kernel,
-        out_shape=pltpu.VMEM((lax.axis_size("tc") * SLOTS, width), F32),
+        out_shape=pltpu.VMEM((len(lines[0]) * SLOTS, width), F32),
         in_specs=[smem()] + [vmem()] * 15,
         out_specs=vmem(),
         scratch_shapes=[pltpu.VMEM((n, width), F32)] * 2,
         compiler_params=params(12),
     )(pinned(flags, pltpu.SMEM), pinned(own), pinned(c_here), pinned(high), pinned(low), pinned(size), *[pinned(b) for b in basis], *got)
-    part = lax.all_to_all(part, "tc", 0, 0, tiled=True)
+    part = lax.all_to_all(part, ("tr", "tc"), 0, 0, tiled=True, axis_index_groups=lines)
     part = pl.pallas_call(
         merge_kernel,
-        out_shape=pltpu.VMEM((lax.axis_size("tr") * SLOTS, width), F32),
+        out_shape=pltpu.VMEM((len(planes[0]) * SLOTS, width), F32),
         in_specs=[vmem()],
         out_specs=vmem(),
     )(pinned(part))
-    part = lax.all_to_all(part, "tr", 0, 0, tiled=True)
+    part = lax.all_to_all(part, ("tr", "tc"), 0, 0, tiled=True, axis_index_groups=planes)
     solution, norm = pl.pallas_call(
         finish_kernel,
         out_shape=[jax.ShapeDtypeStruct((n, width), F32), jax.ShapeDtypeStruct((1, width), F32)],

time: 113 us -> 114 us (level)
  waiting for transfers between devices: 21.3 us -> 8.34 us
  blocking collectives: 30.7 us -> 40.5 us
  starting transfers between devices: 28.6 us -> 32 us
    ppermute x15, waiting for transfers between devices: 21.3 us -> 8.34 us  [exchange(): lax.ppermute(v, *route)]
    all_to_all x2, blocking collectives: 30.7 us -> 40.5 us  [the longest x1 20.3 us: body(): lax.all_to_all(part, ('tr', 'tc'), 0, 0, tiled=True, axis_index_groups=li...]
    ppermute x15, starting transfers between devices: 28.6 us -> 32 us  [exchange(): lax.ppermute(v, *route)]
    pallas_call x2 -> x3, Pallas kernels: 2.51 us -> 3.23 us  [the longest x1 2.46 us: body(): pl.pallas_call(last_kernel, out_shape=pltpu.VMEM((len(lines[0]) * SLOTS,...]
  transfers between devices with their start and end apart: 15 -> 15, of which waited for: 3 -> 5; matrix products, arithmetic and copies ran while one was open for 0% -> 0% of each run, Pallas kernels for 16% -> 6%
where the time goes in v2:
time: 114 us; the launch traced here: 113 us
  blocking collectives  40.5 us (36%)
  starting transfers between devices  32 us (28%)
  Pallas kernels  31 us (27%)
  waiting for transfers between devices  8.34 us (7%)
  between operations  1.46 us (1%)
    ppermute x15, starting transfers between devices, exchange(): lax.ppermute(v, *route)  32 us
    all_to_all x1, blocking collectives, body(): lax.all_to_all(part, ('tr', 'tc'), 0, 0, tiled=True, axis_index_groups=li...  20.3 us
    all_to_all x1, blocking collectives, body(): lax.all_to_all(part, ('tr', 'tc'), 0, 0, tiled=True, axis_index_groups=pl...  20.2 us
    pallas_call x1, Pallas kernels, factor(): pl.pallas_call(factor_kernel, out_shape=[pltpu.VMEM((n, n), F32), square,...  12.9 us
    ppermute x15, waiting for transfers between devices, exchange(): lax.ppermute(v, *route)  8.34 us
    pallas_call x2, Pallas kernels, body(): pl.pallas_call(step_kernel, out_shape=[pltpu.VMEM((n, width), F32)] * 2 +...  5.09 us
    pallas_call x1, Pallas kernels, build(): pl.pallas_call(build_kernel, out_shape=[pltpu.VMEM((n, n), BF16), pltpu.V...  3.8 us
    pallas_call x1, Pallas kernels, first_messages(): pl.pallas_call(functools.partial(message_kernel, last), out_shape=[pltpu....  2.81 us
  transfers between devices with their start and end apart: 15, of which 5 were waited for; matrix products, arithmetic and copies ran while one was open for 0% of the time, Pallas kernels for 6%

profile of v2, /device:TPU:1, one launch (start us, length us, event | category | flops | bytes accessed | tf_op | source)
XLA Modules:
  0.0 113.3 jit_solution(10665949899339005518)
XLA Ops:
  1.3 12.9 %shard_map.68 = (f32[1024,1024]{1,0:T(8,128)S(1)}, bf16[1024,1024]{1,0:T(8,128)(2,1)S(1)}, bf16[1024,1024]{1,0:T(8,128)(2,1)S(1)}, bf16[1024,1024]{1,0:T(8,128)(...) custom-call(s32[1,1]{1,0:T(1,128)S(6)} %copy.7.time, f32[1024,1024]{1,0:T(8,128)} %bitcast.14, ...), custom_call_target="tpu_custom_call" | custom-call | tf_op jit(solution)/shard_map/pallas_call | solution.py:298
  14.2 3.3 %collective-permute-start.2 = (s32[1,1]{1,0:T(1,128)}, s32[1,1]{1,0:T(1,128)}, u32[]{:S(2)}, u32[]{:S(2)}) collective-permute-start(s32[1,1]{1,0:T(1,128)} %get-tuple-element.33.own), channel_id=1, source_target_pairs={{0,1},{1,0},{2,3},{3,2},{4,5},{5,4},{6,7},{7,6},{8,9},{9,8},{10,11... | collective-permute-start | bytes 20 | tf_op jit(solution)/shard_map/ppermute | solution.py:560
  17.5 3.5 %collective-permute-start = (s32[1,1]{1,0:T(1,128)}, s32[1,1]{1,0:T(1,128)}, u32[]{:S(2)}, u32[]{:S(2)}) collective-permute-start(s32[1,1]{1,0:T(1,128)} %get-tuple-element.33.own), channel_id=1, source_target_pairs={{1,2},{3,4},{5,6},{7,8},{9,10},{11,12},{13,14},{2,1},{4,3},{6,5},{... | collective-permute-start | bytes 20 | tf_op jit(solution)/shard_map/ppermute | solution.py:560
  21.0 0.7 shard_map.69
  21.7 0.0 collective-permute-done.1.t2
  21.7 0.7 collective-permute-done.t1
  22.4 2.8 %shard_map.70 = (s32[1,8]{1,0:T(1,128)S(4)}, bf16[1024,128]{1,0:T(8,128)(2,1)S(1)}, bf16[1024,128]{1,0:T(8,128)(2,1)S(1)}, bf16[1024,128]{1,0:T(8,128)(2,1)S(1)}, bf16[1024,128]{1,0:T(8,128)(2,1)S(1)}) custom-call(s32[1,1]{1,0:T(1,128)} %get-tuple-element.33.own, s32[1,1]{1,0:T(1,128)} %collective-permute-done.t1, s32[1,1]{1,0:T(1,128)} %collective-permute-done.1.t2, ...), custom_call_target="tpu_custom_call" | custom-call | tf_op jit(solution)/shard_map/pallas_call | solution.py:343
  25.3 0.7 collective-permute-start.3
  25.9 3.4 %collective-permute-start.4 = (bf16[1024,128]{1,0:T(8,128)(2,1)S(1)}, bf16[1024,128]{1,0:T(8,128)(2,1)S(1)}, u32[]{:S(2)}, u32[]{:S(2)}) collective-permute-start(bf16[1024,128]{1,0:T(8,128)(2,1)S(1)} %get-tuple-element.45), channel_id=1, source_target_pairs={{1,2},{3,4},{5,6},{7,8},{9,10},{11,12},{13,14},{2,1},{4,3},{6,5},{... | collective-permute-start | bytes 786440 | tf_op jit(solution)/shard_map/ppermute | solution.py:560
  29.4 4.9 %collective-permute-start.5 = (bf16[1024,128]{1,0:T(8,128)(2,1)S(1)}, bf16[1024,128]{1,0:T(8,128)(2,1)S(1)}, u32[]{:S(2)}, u32[]{:S(2)}) collective-permute-start(bf16[1024,128]{1,0:T(8,128)(2,1)S(1)} %get-tuple-element.46), channel_id=1, source_target_pairs={{0,16},{16,0},{32,48},{48,32},{64,80},{80,64},{96,112},{112,96},{1... | collective-permute-start | bytes 786440 | tf_op jit(solution)/shard_map/ppermute | solution.py:560
  34.3 3.8 %shard_map.72 = (bf16[1024,1024]{1,0:T(8,128)(2,1)S(1)}, bf16[1024,1024]{1,0:T(8,128)(2,1)S(1)}, f32[8,128]{1,0:T(8,128)S(1)}) custom-call(f32[1024,1024]{1,0:T(8,128)S(1)} %get-tuple-element.41.work), custom_call_target="tpu_custom_call" | custom-call | tf_op jit(solution)/shard_map/pallas_call | solution.py:378
  38.1 0.7 shard_map.71.own_ref
  38.8 1.5 %collective-permute-done.4.g1 = bf16[1024,128]{1,0:T(8,128)(2,1)S(1)} collective-permute-done((bf16[1024,128]{1,0:T(8,128)(2,1)S(1)}, bf16[1024,128]{1,0:T(8,128)(2,1)S(1)}, u32[]{:S(2)}, u32[]{:S(2)}) %collective-permute-start.4) | collective-permute-done | bytes 262176 | tf_op jit(solution)/shard_map/ppermute | solution.py:560
  40.3 2.5 %shard_map.73 = (f32[1024,128]{1,0:T(8,128)S(1)}, f32[1024,128]{1,0:T(8,128)S(1)}, bf16[1024,128]{1,0:T(8,128)(2,1)S(1)}, bf16[1024,128]{1,0:T(8,128)(2,1)S(1)},...) custom-call(s32[1,8]{1,0:T(1,128)S(4)} %get-tuple-element.38.flags, f32[1024,128]{1,0:T(8,128)S(1)} %shard_map.71.own_ref, ...), custom_call_target="tpu_custom_call" | custom-call | tf_op jit(solution)/shard_map/pallas_call | solution.py:598
  42.9 0.7 collective-permute-start.7
  43.6 3.0 %collective-permute-start.8 = (bf16[1024,128]{1,0:T(8,128)(2,1)S(1)}, bf16[1024,128]{1,0:T(8,128)(2,1)S(1)}, u32[]{:S(2)}, u32[]{:S(2)}) collective-permute-start(bf16[1024,128]{1,0:T(8,128)(2,1)S(1)} %get-tuple-element.50), channel_id=1, source_target_pairs={{1,2},{3,4},{5,6},{7,8},{9,10},{11,12},{13,14},{2,1},{4,3},{6,5},{... | collective-permute-start | bytes 786440 | tf_op jit(solution)/shard_map/ppermute | solution.py:560
  46.5 5.2 %collective-permute-start.9 = (bf16[1024,128]{1,0:T(8,128)(2,1)S(1)}, bf16[1024,128]{1,0:T(8,128)(2,1)S(1)}, u32[]{:S(2)}, u32[]{:S(2)}) collective-permute-start(bf16[1024,128]{1,0:T(8,128)(2,1)S(1)} %get-tuple-element.51), channel_id=1, source_target_pairs={{0,16},{16,0},{32,48},{48,32},{64,80},{80,64},{96,112},{112,96},{1... | collective-permute-start | bytes 786440 | tf_op jit(solution)/shard_map/ppermute | solution.py:560
  51.7 0.0 collective-permute-start.10
  51.7 0.7 shard_map.74.own_ref
  52.5 3.0 %collective-permute-done.9.g2 = bf16[1024,128]{1,0:T(8,128)(2,1)S(1)} collective-permute-done((bf16[1024,128]{1,0:T(8,128)(2,1)S(1)}, bf16[1024,128]{1,0:T(8,128)(2,1)S(1)}, u32[]{:S(2)}, u32[]{:S(2)}) %collective-permute-start.9) | collective-permute-done | bytes 262176 | tf_op jit(solution)/shard_map/ppermute | solution.py:560
  55.5 2.5 %shard_map.75 = (f32[1024,128]{1,0:T(8,128)S(1)}, f32[1024,128]{1,0:T(8,128)S(1)}, bf16[1024,128]{1,0:T(8,128)(2,1)S(1)}, bf16[1024,128]{1,0:T(8,128)(2,1)S(1)},...) custom-call(s32[1,8]{1,0:T(1,128)S(4)} %get-tuple-element.38.flags, f32[1024,128]{1,0:T(8,128)S(1)} %shard_map.74.own_ref, ...), custom_call_target="tpu_custom_call" | custom-call | tf_op jit(solution)/shard_map/pallas_call | solution.py:598
  58.0 0.7 collective-permute-start.11
  58.7 3.3 %collective-permute-start.12 = (bf16[1024,128]{1,0:T(8,128)(2,1)S(1)}, bf16[1024,128]{1,0:T(8,128)(2,1)S(1)}, u32[]{:S(2)}, u32[]{:S(2)}) collective-permute-start(bf16[1024,128]{1,0:T(8,128)(2,1)S(1)} %get-tuple-element.59), channel_id=1, source_target_pairs={{1,2},{3,4},{5,6},{7,8},{9,10},{11,12},{13,14},{2,1},{4,3},{6,5},{... | collective-permute-start | bytes 786440 | tf_op jit(solution)/shard_map/ppermute | solution.py:560
  62.1 3.4 %collective-permute-start.13 = (bf16[1024,128]{1,0:T(8,128)(2,1)S(1)}, bf16[1024,128]{1,0:T(8,128)(2,1)S(1)}, u32[]{:S(2)}, u32[]{:S(2)}) collective-permute-start(bf16[1024,128]{1,0:T(8,128)(2,1)S(1)} %get-tuple-element.60), channel_id=1, source_target_pairs={{0,16},{16,0},{32,48},{48,32},{64,80},{80,64},{96,112},{112,96},{1... | collective-permute-start | bytes 786440 | tf_op jit(solution)/shard_map/ppermute | solution.py:560
  65.4 0.7 shard_map.76.own_ref
  66.2 0.2 collective-permute-done.12.g1
  66.4 2.8 %collective-permute-done.13.g2 = bf16[1024,128]{1,0:T(8,128)(2,1)S(1)} collective-permute-done((bf16[1024,128]{1,0:T(8,128)(2,1)S(1)}, bf16[1024,128]{1,0:T(8,128)(2,1)S(1)}, u32[]{:S(2)}, u32[]{:S(2)}) %collective-permute-start.13) | collective-permute-done | bytes 262176 | tf_op jit(solution)/shard_map/ppermute | solution.py:560
  69.2 2.5 %shard_map.77 = f32[256,128]{1,0:T(8,128)S(1)} custom-call(s32[1,8]{1,0:T(1,128)S(4)} %get-tuple-element.38.flags, f32[1024,128]{1,0:T(8,128)S(1)} %shard_map.76.own_ref, bf16[1024,1024]{1,0:T(8,128)(2,1)S(1)} %get-tuple-element.40.c_ref, bf16[1024,1024]{1,0:T(8,128)(2,1)S(1)} %get-tuple-element.42.high_ref, ...), custom_call_target="tpu_custom_call" | custom-call | tf_op jit(solution)/shard_map/pallas_call | solution.py:609
  71.7 20.3 %all_to_all.22 = f32[16,16,128]{2,1,0:T(8,128)S(1)} all-to-all(f32[16,16,128]{2,1,0:T(8,128)S(1)} %bitcast.13), channel_id=1, replica_groups={{0,1,16,17,32,33,48,49,64,65,80,81,96,97,112,113},{2,3,18,19,34,35,50,5..., dimensions={0} | all-to-all | bytes 262144 | tf_op jit(solution)/shard_map/all_to_all | solution.py:617
  92.0 0.1 shard_map.78
  92.1 20.2 %all_to_all.23 = f32[16,16,128]{2,1,0:T(8,128)S(1)} all-to-all(f32[16,16,128]{2,1,0:T(8,128)S(1)} %bitcast.11), channel_id=1, replica_groups={{0,2,4,6,8,10,12,14,128,130,132,134,136,138,140,142},{1,3,5,7,9,11,13,1..., dimensions={0} | all-to-all | bytes 262144 | tf_op jit(solution)/shard_map/all_to_all | solution.py:624
  112.2 1.1 shard_map.79
  (12 shorter events, 0.0 us)
Async XLA Ops:
  14.2 7.5 %collective-permute-start.2 = (s32[1,1]{1,0:T(1,128)}, s32[1,1]{1,0:T(1,128)}, u32[]{:S(2)}, u32[]{:S(2)}) collective-permute-start(s32[1,1]{1,0:T(1,128)} %get-tuple-element.33.own), channel_id=1, source_target_pairs={{0,1},{1,0},{2,3},{3,2},{4,5},{5,4},{6,7},{7,6},{8,9},{9,8},{10,11... | collective-permute-start | bytes 20 | tf_op jit(solution)/shard_map/ppermute | solution.py:560
  17.5 4.2 %collective-permute-start.1 = (s32[1,1]{1,0:T(1,128)}, s32[1,1]{1,0:T(1,128)}, u32[]{:S(2)}, u32[]{:S(2)}) collective-permute-start(s32[1,1]{1,0:T(1,128)} %get-tuple-element.33.own), channel_id=1, source_target_pairs={{0,16},{16,0},{32,48},{48,32},{64,80},{80,64},{96,112},{112,96},{1... | collective-permute-start | bytes 20 | tf_op jit(solution)/shard_map/ppermute | solution.py:560
  17.5 4.9 %collective-permute-start = (s32[1,1]{1,0:T(1,128)}, s32[1,1]{1,0:T(1,128)}, u32[]{:S(2)}, u32[]{:S(2)}) collective-permute-start(s32[1,1]{1,0:T(1,128)} %get-tuple-element.33.own), channel_id=1, source_target_pairs={{1,2},{3,4},{5,6},{7,8},{9,10},{11,12},{13,14},{2,1},{4,3},{6,5},{... | collective-permute-start | bytes 20 | tf_op jit(solution)/shard_map/ppermute | solution.py:560
  25.3 13.5 %collective-permute-start.3 = (bf16[1024,128]{1,0:T(8,128)(2,1)S(1)}, bf16[1024,128]{1,0:T(8,128)(2,1)S(1)}, u32[]{:S(2)}, u32[]{:S(2)}) collective-permute-start(bf16[1024,128]{1,0:T(8,128)(2,1)S(1)} %get-tuple-element.44), channel_id=1, source_target_pairs={{16,32},{48,64},{80,96},{112,128},{144,160},{176,192},{208,224},{3... | collective-permute-start | bytes 786440 | tf_op jit(solution)/shard_map/ppermute | solution.py:560
  25.9 14.4 %collective-permute-start.4 = (bf16[1024,128]{1,0:T(8,128)(2,1)S(1)}, bf16[1024,128]{1,0:T(8,128)(2,1)S(1)}, u32[]{:S(2)}, u32[]{:S(2)}) collective-permute-start(bf16[1024,128]{1,0:T(8,128)(2,1)S(1)} %get-tuple-element.45), channel_id=1, source_target_pairs={{1,2},{3,4},{5,6},{7,8},{9,10},{11,12},{13,14},{2,1},{4,3},{6,5},{... | collective-permute-start | bytes 786440 | tf_op jit(solution)/shard_map/ppermute | solution.py:560
  29.4 10.9 %collective-permute-start.5 = (bf16[1024,128]{1,0:T(8,128)(2,1)S(1)}, bf16[1024,128]{1,0:T(8,128)(2,1)S(1)}, u32[]{:S(2)}, u32[]{:S(2)}) collective-permute-start(bf16[1024,128]{1,0:T(8,128)(2,1)S(1)} %get-tuple-element.46), channel_id=1, source_target_pairs={{0,16},{16,0},{32,48},{48,32},{64,80},{80,64},{96,112},{112,96},{1... | collective-permute-start | bytes 786440 | tf_op jit(solution)/shard_map/ppermute | solution.py:560
  34.3 6.1 %collective-permute-start.6 = (bf16[1024,128]{1,0:T(8,128)(2,1)S(1)}, bf16[1024,128]{1,0:T(8,128)(2,1)S(1)}, u32[]{:S(2)}, u32[]{:S(2)}) collective-permute-start(bf16[1024,128]{1,0:T(8,128)(2,1)S(1)} %get-tuple-element.47), channel_id=1, source_target_pairs={{0,1},{1,0},{2,3},{3,2},{4,5},{5,4},{6,7},{7,6},{8,9},{9,8},{10,11... | collective-permute-start | bytes 786440 | tf_op jit(solution)/shard_map/ppermute | solution.py:560
  42.9 9.6 %collective-permute-start.7 = (bf16[1024,128]{1,0:T(8,128)(2,1)S(1)}, bf16[1024,128]{1,0:T(8,128)(2,1)S(1)}, u32[]{:S(2)}, u32[]{:S(2)}) collective-permute-start(bf16[1024,128]{1,0:T(8,128)(2,1)S(1)} %get-tuple-element.49), channel_id=1, source_target_pairs={{16,32},{48,64},{80,96},{112,128},{144,160},{176,192},{208,224},{3... | collective-permute-start | bytes 786440 | tf_op jit(solution)/shard_map/ppermute | solution.py:560
  43.6 8.9 %collective-permute-start.8 = (bf16[1024,128]{1,0:T(8,128)(2,1)S(1)}, bf16[1024,128]{1,0:T(8,128)(2,1)S(1)}, u32[]{:S(2)}, u32[]{:S(2)}) collective-permute-start(bf16[1024,128]{1,0:T(8,128)(2,1)S(1)} %get-tuple-element.50), channel_id=1, source_target_pairs={{1,2},{3,4},{5,6},{7,8},{9,10},{11,12},{13,14},{2,1},{4,3},{6,5},{... | collective-permute-start | bytes 786440 | tf_op jit(solution)/shard_map/ppermute | solution.py:560
  46.5 8.9 %collective-permute-start.9 = (bf16[1024,128]{1,0:T(8,128)(2,1)S(1)}, bf16[1024,128]{1,0:T(8,128)(2,1)S(1)}, u32[]{:S(2)}, u32[]{:S(2)}) collective-permute-start(bf16[1024,128]{1,0:T(8,128)(2,1)S(1)} %get-tuple-element.51), channel_id=1, source_target_pairs={{0,16},{16,0},{32,48},{48,32},{64,80},{80,64},{96,112},{112,96},{1... | collective-permute-start | bytes 786440 | tf_op jit(solution)/shard_map/ppermute | solution.py:560
  51.7 3.8 %collective-permute-start.10 = (bf16[1024,128]{1,0:T(8,128)(2,1)S(1)}, bf16[1024,128]{1,0:T(8,128)(2,1)S(1)}, u32[]{:S(2)}, u32[]{:S(2)}) collective-permute-start(bf16[1024,128]{1,0:T(8,128)(2,1)S(1)} %get-tuple-element.52), channel_id=1, source_target_pairs={{0,1},{1,0},{2,3},{3,2},{4,5},{5,4},{6,7},{7,6},{8,9},{9,8},{10,11... | collective-permute-start | bytes 786440 | tf_op jit(solution)/shard_map/ppermute | solution.py:560
  58.0 8.1 %collective-permute-start.11 = (bf16[1024,128]{1,0:T(8,128)(2,1)S(1)}, bf16[1024,128]{1,0:T(8,128)(2,1)S(1)}, u32[]{:S(2)}, u32[]{:S(2)}) collective-permute-start(bf16[1024,128]{1,0:T(8,128)(2,1)S(1)} %get-tuple-element.58), channel_id=1, source_target_pairs={{16,32},{48,64},{80,96},{112,128},{144,160},{176,192},{208,224},{3... | collective-permute-start | bytes 786440 | tf_op jit(solution)/shard_map/ppermute | solution.py:560
  58.7 7.7 %collective-permute-start.12 = (bf16[1024,128]{1,0:T(8,128)(2,1)S(1)}, bf16[1024,128]{1,0:T(8,128)(2,1)S(1)}, u32[]{:S(2)}, u32[]{:S(2)}) collective-permute-start(bf16[1024,128]{1,0:T(8,128)(2,1)S(1)} %get-tuple-element.59), channel_id=1, source_target_pairs={{1,2},{3,4},{5,6},{7,8},{9,10},{11,12},{13,14},{2,1},{4,3},{6,5},{... | collective-permute-start | bytes 786440 | tf_op jit(solution)/shard_map/ppermute | solution.py:560
  62.1 7.1 %collective-permute-start.13 = (bf16[1024,128]{1,0:T(8,128)(2,1)S(1)}, bf16[1024,128]{1,0:T(8,128)(2,1)S(1)}, u32[]{:S(2)}, u32[]{:S(2)}) collective-permute-start(bf16[1024,128]{1,0:T(8,128)(2,1)S(1)} %get-tuple-element.60), channel_id=1, source_target_pairs={{0,16},{16,0},{32,48},{48,32},{64,80},{80,64},{96,112},{112,96},{1... | collective-permute-start | bytes 786440 | tf_op jit(solution)/shard_map/ppermute | solution.py:560
  65.4 3.8 %collective-permute-start.14 = (bf16[1024,128]{1,0:T(8,128)(2,1)S(1)}, bf16[1024,128]{1,0:T(8,128)(2,1)S(1)}, u32[]{:S(2)}, u32[]{:S(2)}) collective-permute-start(bf16[1024,128]{1,0:T(8,128)(2,1)S(1)} %get-tuple-element.61), channel_id=1, source_target_pairs={{0,1},{1,0},{2,3},{3,2},{4,5},{5,4},{6,7},{7,6},{8,9},{9,8},{10,11... | collective-permute-start | bytes 786440 | tf_op jit(solution)/shard_map/ppermute | solution.py:560

commit v3 on v2

--- a/solution.py
+++ b/solution.py
@@ -114,10 +114,28 @@
             pending.pop(0)()
 
 
+def combine_rows(blocks, at, work, vec, ahead):
+    tail = blocks - 1
+
+    def begin():
+        ahead[tail - 1] = split(work[at[tail - 1], at[tail]])
+
+    def combine(k):
+        factor_row = work[at[k], at[tail]]
+        for j in range(k + 1, tail):
+            scaled = split(work[at[k], at[j]])
+            factor_row = factor_row - mm3(scaled, ahead[j])
+            vec[at[k], :] = vec[at[k], :] - mm3(scaled, split(vec[at[j], :]))
+        ahead[k] = split(factor_row)
+
+    return [begin] + [functools.partial(combine, k) for k in reversed(range(tail - 1))]
+
+
 def eliminate(n, work, vec, extra, before, after):
     blocks = n // LEAF
     at = [pl.ds(k * LEAF, LEAF) for k in range(blocks)]
     worst = jnp.zeros((1, 1), F32)
+    ahead = {}
     pending = []
     for k in range(blocks):
         before(k)
@@ -161,13 +179,13 @@
             pending.append(functools.partial(push, i))
         pending.append(solve)
         pending += extra(k)
+        if k == blocks - 2:
+            pending += combine_rows(blocks, at, work, vec, ahead)
     for task in pending:
         task()
-    for k in reversed(range(blocks - 1)):
-        total = vec[at[k], :]
-        for j in range(k + 1, blocks):
-            total = total - mm3(split(work[at[k], at[j]]), split(vec[at[j], :]))
-        vec[at[k], :] = total
+    final = split(vec[at[-1], :])
+    for k in range(blocks - 1):
+        vec[at[k], :] = vec[at[k], :] - mm3(ahead[k], final)
     return worst
 
 
@@ -297,7 +315,7 @@
     column = pltpu.VMEM((n, width), F32)
     return pl.pallas_call(
         factor_kernel,
-        out_shape=[pltpu.VMEM((n, n), F32), square, square, square, column, column, jax.ShapeDtypeStruct(time.shape, jnp.int32)],
+        out_shape=[pltpu.VMEM((n, n), F32), square, square, square, column, column, pltpu.VMEM((8, 128), jnp.int32)],
         in_specs=[smem()] + [outside()] * 4,
         out_specs=[vmem()] * 7,
         scratch_shapes=[pltpu.VMEM((LEAF, n), F32), pltpu.SemaphoreType.DMA((n // LEAF + 4,))],

time: 114 us -> 111 us (0.974)
  Pallas kernels: 31 us -> 27.9 us
    pallas_call x1, Pallas kernels: 2.81 us -> 0.45 us  [first_messages(): pl.pallas_call(functools.partial(message_kernel, last), out_shape=[pltpu....]
where the time goes in v3:
time: 111 us; the launch traced here: 110 us
  blocking collectives  40.8 us (37%)
  starting transfers between devices  32 us (29%)
  Pallas kernels  27.9 us (25%)
  waiting for transfers between devices  8.27 us (7%)
  between operations  1.46 us (1%)
    ppermute x15, starting transfers between devices, exchange(): lax.ppermute(v, *route)  32 us
    all_to_all x1, blocking collectives, body(): lax.all_to_all(part, ('tr', 'tc'), 0, 0, tiled=True, axis_index_groups=li...  20.4 us
    all_to_all x1, blocking collectives, body(): lax.all_to_all(part, ('tr', 'tc'), 0, 0, tiled=True, axis_index_groups=pl...  20.4 us
    pallas_call x1, Pallas kernels, factor(): pl.pallas_call(factor_kernel, out_shape=[pltpu.VMEM((n, n), F32), square,...  12.1 us
    ppermute x15, waiting for transfers between devices, exchange(): lax.ppermute(v, *route)  8.27 us
    pallas_call x2, Pallas kernels, body(): pl.pallas_call(step_kernel, out_shape=[pltpu.VMEM((n, width), F32)] * 2 +...  5.09 us
    pallas_call x1, Pallas kernels, build(): pl.pallas_call(build_kernel, out_shape=[pltpu.VMEM((n, n), BF16), pltpu.V...  3.8 us
    pallas_call x1, Pallas kernels, body(): pl.pallas_call(last_kernel, out_shape=pltpu.VMEM((len(lines[0]) * SLOTS,...  2.46 us
  transfers between devices with their start and end apart: 15, of which 5 were waited for; matrix products, arithmetic and copies ran while one was open for 0% of the time, Pallas kernels for 6%

profile of v3, /device:TPU:1, one launch (start us, length us, event | category | flops | bytes accessed | tf_op | source)
XLA Modules:
  0.0 110.5 jit_solution(13911660367748670315)
XLA Ops:
  1.3 12.1 %shard_map.68 = (f32[1024,1024]{1,0:T(8,128)S(1)}, bf16[1024,1024]{1,0:T(8,128)(2,1)S(1)}, bf16[1024,1024]{1,0:T(8,128)(2,1)S(1)}, bf16[1024,1024]{1,0:T(8,128)(...) custom-call(s32[1,1]{1,0:T(1,128)S(6)} %copy.7.time, f32[1024,1024]{1,0:T(8,128)} %bitcast.14, ...), custom_call_target="tpu_custom_call" | custom-call | tf_op jit(solution)/shard_map/pallas_call | solution.py:316
  13.4 3.3 %collective-permute-start.2 = (s32[8,128]{1,0:T(8,128)S(1)}, s32[8,128]{1,0:T(8,128)S(1)}, u32[]{:S(2)}, u32[]{:S(2)}) collective-permute-start(s32[8,128]{1,0:T(8,128)S(1)} %get-tuple-element.33.own), channel_id=1, source_target_pairs={{0,1},{1,0},{2,3},{3,2},{4,5},{5,4},{6,7},{7,6},{8,9},{9,8},{10,11... | collective-permute-start | bytes 12296 | tf_op jit(solution)/shard_map/ppermute | solution.py:578
  16.8 0.0 collective-permute-start.1
  16.8 3.5 %collective-permute-start = (s32[8,128]{1,0:T(8,128)S(1)}, s32[8,128]{1,0:T(8,128)S(1)}, u32[]{:S(2)}, u32[]{:S(2)}) collective-permute-start(s32[8,128]{1,0:T(8,128)S(1)} %get-tuple-element.33.own), channel_id=1, source_target_pairs={{1,2},{3,4},{5,6},{7,8},{9,10},{11,12},{13,14},{2,1},{4,3},{6,5},{... | collective-permute-start | bytes 12296 | tf_op jit(solution)/shard_map/ppermute | solution.py:578
  20.2 0.7 shard_map.69
  21.0 0.7 collective-permute-done.t1
  21.7 0.5 shard_map.70
  22.1 0.7 collective-permute-start.3
  22.8 3.5 %collective-permute-start.4 = (bf16[1024,128]{1,0:T(8,128)(2,1)S(1)}, bf16[1024,128]{1,0:T(8,128)(2,1)S(1)}, u32[]{:S(2)}, u32[]{:S(2)}) collective-permute-start(bf16[1024,128]{1,0:T(8,128)(2,1)S(1)} %get-tuple-element.45), channel_id=1, source_target_pairs={{1,2},{3,4},{5,6},{7,8},{9,10},{11,12},{13,14},{2,1},{4,3},{6,5},{... | collective-permute-start | bytes 786440 | tf_op jit(solution)/shard_map/ppermute | solution.py:578
  26.3 4.9 %collective-permute-start.5 = (bf16[1024,128]{1,0:T(8,128)(2,1)S(1)}, bf16[1024,128]{1,0:T(8,128)(2,1)S(1)}, u32[]{:S(2)}, u32[]{:S(2)}) collective-permute-start(bf16[1024,128]{1,0:T(8,128)(2,1)S(1)} %get-tuple-element.46), channel_id=1, source_target_pairs={{0,16},{16,0},{32,48},{48,32},{64,80},{80,64},{96,112},{112,96},{1... | collective-permute-start | bytes 786440 | tf_op jit(solution)/shard_map/ppermute | solution.py:578
  31.2 3.8 %shard_map.72 = (bf16[1024,1024]{1,0:T(8,128)(2,1)S(1)}, bf16[1024,1024]{1,0:T(8,128)(2,1)S(1)}, f32[8,128]{1,0:T(8,128)S(1)}) custom-call(f32[1024,1024]{1,0:T(8,128)S(1)} %get-tuple-element.41.work), custom_call_target="tpu_custom_call" | custom-call | tf_op jit(solution)/shard_map/pallas_call | solution.py:396
  35.0 0.7 shard_map.71.own_ref
  35.7 1.5 %collective-permute-done.4.g1 = bf16[1024,128]{1,0:T(8,128)(2,1)S(1)} collective-permute-done((bf16[1024,128]{1,0:T(8,128)(2,1)S(1)}, bf16[1024,128]{1,0:T(8,128)(2,1)S(1)}, u32[]{:S(2)}, u32[]{:S(2)}) %collective-permute-start.4) | collective-permute-done | bytes 262176 | tf_op jit(solution)/shard_map/ppermute | solution.py:578
  37.2 2.5 %shard_map.73 = (f32[1024,128]{1,0:T(8,128)S(1)}, f32[1024,128]{1,0:T(8,128)S(1)}, bf16[1024,128]{1,0:T(8,128)(2,1)S(1)}, bf16[1024,128]{1,0:T(8,128)(2,1)S(1)},...) custom-call(s32[1,8]{1,0:T(1,128)S(4)} %get-tuple-element.38.flags, f32[1024,128]{1,0:T(8,128)S(1)} %shard_map.71.own_ref, ...), custom_call_target="tpu_custom_call" | custom-call | tf_op jit(solution)/shard_map/pallas_call | solution.py:616
  39.7 0.7 collective-permute-start.7
  40.4 3.0 %collective-permute-start.8 = (bf16[1024,128]{1,0:T(8,128)(2,1)S(1)}, bf16[1024,128]{1,0:T(8,128)(2,1)S(1)}, u32[]{:S(2)}, u32[]{:S(2)}) collective-permute-start(bf16[1024,128]{1,0:T(8,128)(2,1)S(1)} %get-tuple-element.50), channel_id=1, source_target_pairs={{1,2},{3,4},{5,6},{7,8},{9,10},{11,12},{13,14},{2,1},{4,3},{6,5},{... | collective-permute-start | bytes 786440 | tf_op jit(solution)/shard_map/ppermute | solution.py:578
  43.5 5.2 %collective-permute-start.9 = (bf16[1024,128]{1,0:T(8,128)(2,1)S(1)}, bf16[1024,128]{1,0:T(8,128)(2,1)S(1)}, u32[]{:S(2)}, u32[]{:S(2)}) collective-permute-start(bf16[1024,128]{1,0:T(8,128)(2,1)S(1)} %get-tuple-element.51), channel_id=1, source_target_pairs={{0,16},{16,0},{32,48},{48,32},{64,80},{80,64},{96,112},{112,96},{1... | collective-permute-start | bytes 786440 | tf_op jit(solution)/shard_map/ppermute | solution.py:578
  48.6 0.0 collective-permute-start.10
  48.6 0.7 shard_map.74.own_ref
  49.4 3.0 %collective-permute-done.9.g2 = bf16[1024,128]{1,0:T(8,128)(2,1)S(1)} collective-permute-done((bf16[1024,128]{1,0:T(8,128)(2,1)S(1)}, bf16[1024,128]{1,0:T(8,128)(2,1)S(1)}, u32[]{:S(2)}, u32[]{:S(2)}) %collective-permute-start.9) | collective-permute-done | bytes 262176 | tf_op jit(solution)/shard_map/ppermute | solution.py:578
  52.4 2.5 %shard_map.75 = (f32[1024,128]{1,0:T(8,128)S(1)}, f32[1024,128]{1,0:T(8,128)S(1)}, bf16[1024,128]{1,0:T(8,128)(2,1)S(1)}, bf16[1024,128]{1,0:T(8,128)(2,1)S(1)},...) custom-call(s32[1,8]{1,0:T(1,128)S(4)} %get-tuple-element.38.flags, f32[1024,128]{1,0:T(8,128)S(1)} %shard_map.74.own_ref, ...), custom_call_target="tpu_custom_call" | custom-call | tf_op jit(solution)/shard_map/pallas_call | solution.py:616
  54.9 0.7 collective-permute-start.11
  55.6 3.3 %collective-permute-start.12 = (bf16[1024,128]{1,0:T(8,128)(2,1)S(1)}, bf16[1024,128]{1,0:T(8,128)(2,1)S(1)}, u32[]{:S(2)}, u32[]{:S(2)}) collective-permute-start(bf16[1024,128]{1,0:T(8,128)(2,1)S(1)} %get-tuple-element.59), channel_id=1, source_target_pairs={{1,2},{3,4},{5,6},{7,8},{9,10},{11,12},{13,14},{2,1},{4,3},{6,5},{... | collective-permute-start | bytes 786440 | tf_op jit(solution)/shard_map/ppermute | solution.py:578
  59.0 3.3 %collective-permute-start.13 = (bf16[1024,128]{1,0:T(8,128)(2,1)S(1)}, bf16[1024,128]{1,0:T(8,128)(2,1)S(1)}, u32[]{:S(2)}, u32[]{:S(2)}) collective-permute-start(bf16[1024,128]{1,0:T(8,128)(2,1)S(1)} %get-tuple-element.60), channel_id=1, source_target_pairs={{0,16},{16,0},{32,48},{48,32},{64,80},{80,64},{96,112},{112,96},{1... | collective-permute-start | bytes 786440 | tf_op jit(solution)/shard_map/ppermute | solution.py:578
  62.3 0.7 shard_map.76.own_ref
  63.0 0.3 collective-permute-done.12.g1
  63.3 2.7 %collective-permute-done.13.g2 = bf16[1024,128]{1,0:T(8,128)(2,1)S(1)} collective-permute-done((bf16[1024,128]{1,0:T(8,128)(2,1)S(1)}, bf16[1024,128]{1,0:T(8,128)(2,1)S(1)}, u32[]{:S(2)}, u32[]{:S(2)}) %collective-permute-start.13) | collective-permute-done | bytes 262176 | tf_op jit(solution)/shard_map/ppermute | solution.py:578
  66.1 2.5 %shard_map.77 = f32[256,128]{1,0:T(8,128)S(1)} custom-call(s32[1,8]{1,0:T(1,128)S(4)} %get-tuple-element.38.flags, f32[1024,128]{1,0:T(8,128)S(1)} %shard_map.76.own_ref, bf16[1024,1024]{1,0:T(8,128)(2,1)S(1)} %get-tuple-element.40.c_ref, bf16[1024,1024]{1,0:T(8,128)(2,1)S(1)} %get-tuple-element.42.high_ref, ...), custom_call_target="tpu_custom_call" | custom-call | tf_op jit(solution)/shard_map/pallas_call | solution.py:627
  68.5 20.4 %all_to_all.22 = f32[16,16,128]{2,1,0:T(8,128)S(1)} all-to-all(f32[16,16,128]{2,1,0:T(8,128)S(1)} %bitcast.13), channel_id=1, replica_groups={{0,1,16,17,32,33,48,49,64,65,80,81,96,97,112,113},{2,3,18,19,34,35,50,5..., dimensions={0} | all-to-all | bytes 262144 | tf_op jit(solution)/shard_map/all_to_all | solution.py:635
  88.9 0.1 shard_map.78
  89.0 20.4 %all_to_all.23 = f32[16,16,128]{2,1,0:T(8,128)S(1)} all-to-all(f32[16,16,128]{2,1,0:T(8,128)S(1)} %bitcast.11), channel_id=1, replica_groups={{0,2,4,6,8,10,12,14,128,130,132,134,136,138,140,142},{1,3,5,7,9,11,13,1..., dimensions={0} | all-to-all | bytes 262144 | tf_op jit(solution)/shard_map/all_to_all | solution.py:642
  109.4 1.1 shard_map.79
  (12 shorter events, 0.0 us)
Async XLA Ops:
  13.4 7.5 %collective-permute-start.2 = (s32[8,128]{1,0:T(8,128)S(1)}, s32[8,128]{1,0:T(8,128)S(1)}, u32[]{:S(2)}, u32[]{:S(2)}) collective-permute-start(s32[8,128]{1,0:T(8,128)S(1)} %get-tuple-element.33.own), channel_id=1, source_target_pairs={{0,1},{1,0},{2,3},{3,2},{4,5},{5,4},{6,7},{7,6},{8,9},{9,8},{10,11... | collective-permute-start | bytes 12296 | tf_op jit(solution)/shard_map/ppermute | solution.py:578
  16.8 4.2 %collective-permute-start.1 = (s32[8,128]{1,0:T(8,128)S(1)}, s32[8,128]{1,0:T(8,128)S(1)}, u32[]{:S(2)}, u32[]{:S(2)}) collective-permute-start(s32[8,128]{1,0:T(8,128)S(1)} %get-tuple-element.33.own), channel_id=1, source_target_pairs={{0,16},{16,0},{32,48},{48,32},{64,80},{80,64},{96,112},{112,96},{1... | collective-permute-start | bytes 12296 | tf_op jit(solution)/shard_map/ppermute | solution.py:578
  16.8 4.9 %collective-permute-start = (s32[8,128]{1,0:T(8,128)S(1)}, s32[8,128]{1,0:T(8,128)S(1)}, u32[]{:S(2)}, u32[]{:S(2)}) collective-permute-start(s32[8,128]{1,0:T(8,128)S(1)} %get-tuple-element.33.own), channel_id=1, source_target_pairs={{1,2},{3,4},{5,6},{7,8},{9,10},{11,12},{13,14},{2,1},{4,3},{6,5},{... | collective-permute-start | bytes 12296 | tf_op jit(solution)/shard_map/ppermute | solution.py:578
  22.1 13.6 %collective-permute-start.3 = (bf16[1024,128]{1,0:T(8,128)(2,1)S(1)}, bf16[1024,128]{1,0:T(8,128)(2,1)S(1)}, u32[]{:S(2)}, u32[]{:S(2)}) collective-permute-start(bf16[1024,128]{1,0:T(8,128)(2,1)S(1)} %get-tuple-element.44), channel_id=1, source_target_pairs={{16,32},{48,64},{80,96},{112,128},{144,160},{176,192},{208,224},{3... | collective-permute-start | bytes 786440 | tf_op jit(solution)/shard_map/ppermute | solution.py:578
  22.8 14.4 %collective-permute-start.4 = (bf16[1024,128]{1,0:T(8,128)(2,1)S(1)}, bf16[1024,128]{1,0:T(8,128)(2,1)S(1)}, u32[]{:S(2)}, u32[]{:S(2)}) collective-permute-start(bf16[1024,128]{1,0:T(8,128)(2,1)S(1)} %get-tuple-element.45), channel_id=1, source_target_pairs={{1,2},{3,4},{5,6},{7,8},{9,10},{11,12},{13,14},{2,1},{4,3},{6,5},{... | collective-permute-start | bytes 786440 | tf_op jit(solution)/shard_map/ppermute | solution.py:578
  26.3 10.9 %collective-permute-start.5 = (bf16[1024,128]{1,0:T(8,128)(2,1)S(1)}, bf16[1024,128]{1,0:T(8,128)(2,1)S(1)}, u32[]{:S(2)}, u32[]{:S(2)}) collective-permute-start(bf16[1024,128]{1,0:T(8,128)(2,1)S(1)} %get-tuple-element.46), channel_id=1, source_target_pairs={{0,16},{16,0},{32,48},{48,32},{64,80},{80,64},{96,112},{112,96},{1... | collective-permute-start | bytes 786440 | tf_op jit(solution)/shard_map/ppermute | solution.py:578
  31.2 6.0 %collective-permute-start.6 = (bf16[1024,128]{1,0:T(8,128)(2,1)S(1)}, bf16[1024,128]{1,0:T(8,128)(2,1)S(1)}, u32[]{:S(2)}, u32[]{:S(2)}) collective-permute-start(bf16[1024,128]{1,0:T(8,128)(2,1)S(1)} %get-tuple-element.47), channel_id=1, source_target_pairs={{0,1},{1,0},{2,3},{3,2},{4,5},{5,4},{6,7},{7,6},{8,9},{9,8},{10,11... | collective-permute-start | bytes 786440 | tf_op jit(solution)/shard_map/ppermute | solution.py:578
  39.7 9.6 %collective-permute-start.7 = (bf16[1024,128]{1,0:T(8,128)(2,1)S(1)}, bf16[1024,128]{1,0:T(8,128)(2,1)S(1)}, u32[]{:S(2)}, u32[]{:S(2)}) collective-permute-start(bf16[1024,128]{1,0:T(8,128)(2,1)S(1)} %get-tuple-element.49), channel_id=1, source_target_pairs={{16,32},{48,64},{80,96},{112,128},{144,160},{176,192},{208,224},{3... | collective-permute-start | bytes 786440 | tf_op jit(solution)/shard_map/ppermute | solution.py:578
  40.4 8.9 %collective-permute-start.8 = (bf16[1024,128]{1,0:T(8,128)(2,1)S(1)}, bf16[1024,128]{1,0:T(8,128)(2,1)S(1)}, u32[]{:S(2)}, u32[]{:S(2)}) collective-permute-start(bf16[1024,128]{1,0:T(8,128)(2,1)S(1)} %get-tuple-element.50), channel_id=1, source_target_pairs={{1,2},{3,4},{5,6},{7,8},{9,10},{11,12},{13,14},{2,1},{4,3},{6,5},{... | collective-permute-start | bytes 786440 | tf_op jit(solution)/shard_map/ppermute | solution.py:578
  43.5 8.9 %collective-permute-start.9 = (bf16[1024,128]{1,0:T(8,128)(2,1)S(1)}, bf16[1024,128]{1,0:T(8,128)(2,1)S(1)}, u32[]{:S(2)}, u32[]{:S(2)}) collective-permute-start(bf16[1024,128]{1,0:T(8,128)(2,1)S(1)} %get-tuple-element.51), channel_id=1, source_target_pairs={{0,16},{16,0},{32,48},{48,32},{64,80},{80,64},{96,112},{112,96},{1... | collective-permute-start | bytes 786440 | tf_op jit(solution)/shard_map/ppermute | solution.py:578
  48.6 3.8 %collective-permute-start.10 = (bf16[1024,128]{1,0:T(8,128)(2,1)S(1)}, bf16[1024,128]{1,0:T(8,128)(2,1)S(1)}, u32[]{:S(2)}, u32[]{:S(2)}) collective-permute-start(bf16[1024,128]{1,0:T(8,128)(2,1)S(1)} %get-tuple-element.52), channel_id=1, source_target_pairs={{0,1},{1,0},{2,3},{3,2},{4,5},{5,4},{6,7},{7,6},{8,9},{9,8},{10,11... | collective-permute-start | bytes 786440 | tf_op jit(solution)/shard_map/ppermute | solution.py:578
  54.9 8.1 %collective-permute-start.11 = (bf16[1024,128]{1,0:T(8,128)(2,1)S(1)}, bf16[1024,128]{1,0:T(8,128)(2,1)S(1)}, u32[]{:S(2)}, u32[]{:S(2)}) collective-permute-start(bf16[1024,128]{1,0:T(8,128)(2,1)S(1)} %get-tuple-element.58), channel_id=1, source_target_pairs={{16,32},{48,64},{80,96},{112,128},{144,160},{176,192},{208,224},{3... | collective-permute-start | bytes 786440 | tf_op jit(solution)/shard_map/ppermute | solution.py:578
  55.6 7.7 %collective-permute-start.12 = (bf16[1024,128]{1,0:T(8,128)(2,1)S(1)}, bf16[1024,128]{1,0:T(8,128)(2,1)S(1)}, u32[]{:S(2)}, u32[]{:S(2)}) collective-permute-start(bf16[1024,128]{1,0:T(8,128)(2,1)S(1)} %get-tuple-element.59), channel_id=1, source_target_pairs={{1,2},{3,4},{5,6},{7,8},{9,10},{11,12},{13,14},{2,1},{4,3},{6,5},{... | collective-permute-start | bytes 786440 | tf_op jit(solution)/shard_map/ppermute | solution.py:578
  59.0 7.1 %collective-permute-start.13 = (bf16[1024,128]{1,0:T(8,128)(2,1)S(1)}, bf16[1024,128]{1,0:T(8,128)(2,1)S(1)}, u32[]{:S(2)}, u32[]{:S(2)}) collective-permute-start(bf16[1024,128]{1,0:T(8,128)(2,1)S(1)} %get-tuple-element.60), channel_id=1, source_target_pairs={{0,16},{16,0},{32,48},{48,32},{64,80},{80,64},{96,112},{112,96},{1... | collective-permute-start | bytes 786440 | tf_op jit(solution)/shard_map/ppermute | solution.py:578
  62.3 3.8 %collective-permute-start.14 = (bf16[1024,128]{1,0:T(8,128)(2,1)S(1)}, bf16[1024,128]{1,0:T(8,128)(2,1)S(1)}, u32[]{:S(2)}, u32[]{:S(2)}) collective-permute-start(bf16[1024,128]{1,0:T(8,128)(2,1)S(1)} %get-tuple-element.61), channel_id=1, source_target_pairs={{0,1},{1,0},{2,3},{3,2},{4,5},{5,4},{6,7},{7,6},{8,9},{9,8},{10,11... | collective-permute-start | bytes 786440 | tf_op jit(solution)/shard_map/ppermute | solution.py:578

commit v4 on v3

--- a/solution.py
+++ b/solution.py
@@ -331,7 +331,7 @@
         back[rows, :] = mm(ct_ref[rows, :], high).astype(BF16)
 
 
-def message_kernel(last, own, t1, t2, t3, ahead, back, flags, m0, m1, m2, m3):
+def message_kernel(last, t3, t2, t1, own, ahead, back, flags, m0, m1, m2, m3):
     here, *times = [jnp.max(t[...]) for t in (own, t1, t2, t3)]
     next_left = here < last
     prev_left = here > 1
@@ -364,7 +364,7 @@
         in_specs=[vmem()] * 6,
         out_specs=[smem()] + [vmem()] * 4,
         compiler_params=params(8),
-    )(*[pinned(t) for t in tags], *[pinned(p) for p in parts])
+    )(*[pinned(t) for t in reversed(tags)], *[pinned(p) for p in parts])
 
 
 def build_kernel(work, high_ref, low_ref, size_ref):
@@ -466,23 +466,46 @@
         out_ref[pl.ds(d, SLOTS), :] = packed
 
 
-def last_kernel(flags, own_ref, c_ref, high_ref, low_ref, size_ref, r0, p0, r1, p1, r2, p2, g0, g1, g2, g3, out_ref, r3, p3):
+def magnitude(ref):
+    return jnp.maximum(jnp.max(jnp.abs(ref[...]), axis=0, keepdims=True), 1e-30)
+
+
+def add_gram(rows, pairs, res, vec, sizes, unit):
+    used_left = sorted({i for i, _ in pairs})
+    used_right = sorted({j for _, j in pairs})
+    left_scale = {i: 1.0 / sizes[i] for i in used_left}
+    right_scale = {j: 1.0 / (sizes[j] * unit) for j in used_right}
+    for pair in pairs:
+        rows[pair] = jnp.zeros_like(unit)
+    for k in range(0, res[0].shape[0], ROWS):
+        at = pl.ds(k, ROWS)
+        left = {i: res[i][at, :] * left_scale[i] for i in used_left}
+        right = {j: vec[j][at, :] * right_scale[j] for j in used_right}
+        for i, j in pairs:
+            rows[i, j] = rows[i, j] + jnp.sum(left[i] * right[j], axis=0, keepdims=True)
+
+
+def early_kernel(diag_ref, size_ref, r0, p0, r1, p1, r2, p2, out_ref, rows_ref):
+    own_kernel(diag_ref, p2, out_ref)
+    res, vec = (r0, r1, r2), (p0, p1, p2)
+    sizes = [magnitude(r) for r in res]
+    rows = {}
+    add_gram(rows, [pair for pair in PAIRS if pair[1] < ITERS], res, vec, sizes, size_ref[0:1, :])
+    listed = [rows[pair] for pair in PAIRS if pair[1] < ITERS] + sizes
+    listed = listed + [jnp.zeros_like(sizes[0])] * (SLOTS - len(listed))
+    rows_ref[...] = jnp.concatenate(listed, axis=0)
+
+
+def last_kernel(flags, own_ref, c_ref, high_ref, low_ref, size_ref, rows_ref, r0, r1, r2, g0, g1, g2, g3, out_ref, r3, p3):
     residual_rows(flags, own_ref, c_ref, (g0, g1, g2, g3), r3)
     store_applied(p3, high_ref, low_ref, r3)
-    res = (r0, r1, r2, r3)
-    vec = (p0, p1, p2, p3)
     unit = size_ref[0:1, :]
-    sizes = [jnp.maximum(jnp.max(jnp.abs(r[...]), axis=0, keepdims=True), 1e-30) for r in res]
-    left_scale = [1.0 / v for v in sizes]
-    right_scale = [1.0 / (v * unit) for v in sizes]
-    rows = [jnp.zeros_like(unit)] * len(PAIRS)
-    for k in range(0, r3.shape[0], LEAF):
-        at = pl.ds(k, LEAF)
-        left = [res[i][at, :] * left_scale[i] for i in range(BASIS)]
-        right = [vec[i][at, :] * right_scale[i] for i in range(BASIS)]
-        for m, (i, j) in enumerate(PAIRS):
-            rows[m] = rows[m] + jnp.sum(left[i] * right[j], axis=0, keepdims=True)
-    pack(rows + sizes + [unit], out_ref)
+    early = [pair for pair in PAIRS if pair[1] < ITERS]
+    rows = {pair: rows_ref[m:m + 1, :] for m, pair in enumerate(early)}
+    sizes = [rows_ref[len(early) + i:len(early) + i + 1, :] for i in range(ITERS)] + [magnitude(r3)]
+    late = [pair for pair in PAIRS if pair[1] == ITERS]
+    add_gram(rows, late, (r0, r1, r2, r3), {ITERS: p3}, sizes, unit)
+    pack([rows[pair] for pair in PAIRS] + sizes + [unit], out_ref)
 
 
 def merge(in_ref):
@@ -575,7 +598,15 @@
     even_r, odd_r = neighbour_perms(lax.axis_size("tr"))
     even_c, odd_c = neighbour_perms(lax.axis_size("tc"))
     routes = (("tr", odd_r), ("tc", odd_c), ("tr", even_r), ("tc", even_c))
-    return [None if v is None else lax.ppermute(v, *route) for v, route in zip(values, routes)]
+    return [lax.ppermute(v, *route) for v, route in zip(values, routes)]
+
+
+def exchange_tags(tag):
+    even_r, _ = neighbour_perms(lax.axis_size("tr"))
+    even_c, odd_c = neighbour_perms(lax.axis_size("tc"))
+    near = lax.ppermute(tag, "tc", even_c)
+    below = lax.ppermute(tag, "tr", even_r)
+    return [lax.ppermute(tag, "tc", odd_c), below, near]
 
 
 def reduce_groups():
@@ -598,20 +629,29 @@
     work, c_here, flipped, diag_here, res, vec, own_tag = factor(
         precond[0, 0], rhs[0, 0], coupling[0, 0], diag_block[0, 0], slot_time
     )
-    tags = [own_tag] + exchange([None] + [own_tag] * 3)[1:]
+    tags = [own_tag] + exchange_tags(own_tag)
     flags, *messages = first_messages(last, tags, flipped, vec)
     basis = [res, vec]
     for step in range(ITERS):
         got = exchange(messages)
         if step == 0:
             high, low, size = build(work, width)
-        own = pl.pallas_call(
-            own_kernel,
-            out_shape=pltpu.VMEM((n, width), F32),
-            in_specs=[vmem()] * 2,
-            out_specs=vmem(),
-            compiler_params=params(8),
-        )(pinned(diag_here), pinned(vec))
+        if step < ITERS - 1:
+            own = pl.pallas_call(
+                own_kernel,
+                out_shape=pltpu.VMEM((n, width), F32),
+                in_specs=[vmem()] * 2,
+                out_specs=vmem(),
+                compiler_params=params(8),
+            )(pinned(diag_here), pinned(vec))
+        else:
+            own, early = pl.pallas_call(
+                early_kernel,
+                out_shape=[pltpu.VMEM((n, width), F32), pltpu.VMEM((SLOTS, width), F32)],
+                in_specs=[vmem()] * 8,
+                out_specs=[vmem()] * 2,
+                compiler_params=params(8),
+            )(pinned(diag_here), pinned(size), *[pinned(b) for b in basis])
         if step < ITERS - 1:
             out = pl.pallas_call(
                 step_kernel,
@@ -627,11 +667,11 @@
     part = pl.pallas_call(
         last_kernel,
         out_shape=pltpu.VMEM((len(lines[0]) * SLOTS, width), F32),
-        in_specs=[smem()] + [vmem()] * 15,
+        in_specs=[smem()] + [vmem()] * 13,
         out_specs=vmem(),
         scratch_shapes=[pltpu.VMEM((n, width), F32)] * 2,
         compiler_params=params(12),
-    )(pinned(flags, pltpu.SMEM), pinned(own), pinned(c_here), pinned(high), pinned(low), pinned(size), *[pinned(b) for b in basis], *got)
+    )(pinned(flags, pltpu.SMEM), pinned(own), pinned(c_here), pinned(high), pinned(low), pinned(size), pinned(early), *[pinned(b) for b in basis[::2]], *got)
     part = lax.all_to_all(part, ("tr", "tc"), 0, 0, tiled=True, axis_index_groups=lines)
     part = pl.pallas_call(
         merge_kernel,

time: 111 us -> 109 us (0.982)
  starting transfers between devices: 32 us -> 30.4 us
    ppermute x15, starting transfers between devices: 32 us -> 30.4 us  [the longest x12 24.1 us: exchange(): return [lax.ppermute(v, *route) for v, route in zip(values, routes)]]
  transfers between devices with their start and end apart: 15 -> 15, of which waited for: 5 -> 6; matrix products, arithmetic and copies ran while one was open for 0% -> 0% of each run, Pallas kernels for 6% -> 6%
where the time goes in v4:
time: 109 us
  blocking collectives  40.2 us (37%)
  starting transfers between devices  30.4 us (28%)
  Pallas kernels  27.9 us (26%)
  waiting for transfers between devices  8.75 us (8%)
  between operations  1.45 us (1%)
    ppermute x12, starting transfers between devices, exchange(): return [lax.ppermute(v, *route) for v, route in zip(values, routes)]  24.1 us
    all_to_all x1, blocking collectives, body(): lax.all_to_all(part, ('tr', 'tc'), 0, 0, tiled=True, axis_index_groups=li...  20.3 us
    all_to_all x1, blocking collectives, body(): lax.all_to_all(part, ('tr', 'tc'), 0, 0, tiled=True, axis_index_groups=pl...  19.9 us
    pallas_call x1, Pallas kernels, factor(): pl.pallas_call(factor_kernel, out_shape=[pltpu.VMEM((n, n), F32), square,...  12.1 us
    ppermute x12, waiting for transfers between devices, exchange(): return [lax.ppermute(v, *route) for v, route in zip(values, routes)]  8.3 us
    pallas_call x2, Pallas kernels, body(): pl.pallas_call(step_kernel, out_shape=[pltpu.VMEM((n, width), F32)] * 2 +...  5.08 us
    ppermute x1, starting transfers between devices, exchange_tags(): return [lax.ppermute(tag, 'tc', odd_c), below, near]  4.51 us
    pallas_call x1, Pallas kernels, build(): pl.pallas_call(build_kernel, out_shape=[pltpu.VMEM((n, n), BF16), pltpu.V...  3.8 us
  transfers between devices with their start and end apart: 15, of which 6 were waited for; matrix products, arithmetic and copies ran while one was open for 0% of the time, Pallas kernels for 6%

profile of v4, /device:TPU:1, one launch (start us, length us, event | category | flops | bytes accessed | tf_op | source)
XLA Modules:
  0.0 108.7 jit_solution(11924532042159367301)
XLA Ops:
  1.3 12.1 %shard_map.68 = (f32[1024,1024]{1,0:T(8,128)S(1)}, bf16[1024,1024]{1,0:T(8,128)(2,1)S(1)}, bf16[1024,1024]{1,0:T(8,128)(2,1)S(1)}, bf16[1024,1024]{1,0:T(8,128)(...) custom-call(s32[1,1]{1,0:T(1,128)S(6)} %copy.7.time, f32[1024,1024]{1,0:T(8,128)} %bitcast.14, ...), custom_call_target="tpu_custom_call" | custom-call | tf_op jit(solution)/shard_map/pallas_call | solution.py:316
  13.4 4.5 %collective-permute-start.2 = (s32[8,128]{1,0:T(8,128)S(1)}, s32[8,128]{1,0:T(8,128)S(1)}, u32[]{:S(2)}, u32[]{:S(2)}) collective-permute-start(s32[8,128]{1,0:T(8,128)S(1)} %get-tuple-element.35.own), channel_id=1, source_target_pairs={{1,2},{3,4},{5,6},{7,8},{9,10},{11,12},{13,14},{2,1},{4,3},{6,5},{... | collective-permute-start | bytes 12296 | tf_op jit(solution)/shard_map/ppermute | solution.py:609
  17.9 1.7 %collective-permute-start.1 = (s32[8,128]{1,0:T(8,128)S(1)}, s32[8,128]{1,0:T(8,128)S(1)}, u32[]{:S(2)}, u32[]{:S(2)}) collective-permute-start(s32[8,128]{1,0:T(8,128)S(1)} %get-tuple-element.35.own), channel_id=1, source_target_pairs={{0,16},{16,0},{32,48},{48,32},{64,80},{80,64},{96,112},{112,96},{1... | collective-permute-start | bytes 12296 | tf_op jit(solution)/shard_map/ppermute | solution.py:608
  19.7 0.0 collective-permute-start
  19.7 0.7 shard_map.69
  20.4 0.3 collective-permute-done.1.t2
  20.7 0.2 collective-permute-done.t3
  20.8 0.5 shard_map.70
  21.3 0.7 collective-permute-start.3
  22.0 3.2 %collective-permute-start.4 = (bf16[1024,128]{1,0:T(8,128)(2,1)S(1)}, bf16[1024,128]{1,0:T(8,128)(2,1)S(1)}, u32[]{:S(2)}, u32[]{:S(2)}) collective-permute-start(bf16[1024,128]{1,0:T(8,128)(2,1)S(1)} %get-tuple-element.49), channel_id=1, source_target_pairs={{1,2},{3,4},{5,6},{7,8},{9,10},{11,12},{13,14},{2,1},{4,3},{6,5},{... | collective-permute-start | bytes 786440 | tf_op jit(solution)/shard_map/ppermute | solution.py:601
  25.2 4.9 %collective-permute-start.5 = (bf16[1024,128]{1,0:T(8,128)(2,1)S(1)}, bf16[1024,128]{1,0:T(8,128)(2,1)S(1)}, u32[]{:S(2)}, u32[]{:S(2)}) collective-permute-start(bf16[1024,128]{1,0:T(8,128)(2,1)S(1)} %get-tuple-element.50), channel_id=1, source_target_pairs={{0,16},{16,0},{32,48},{48,32},{64,80},{80,64},{96,112},{112,96},{1... | collective-permute-start | bytes 786440 | tf_op jit(solution)/shard_map/ppermute | solution.py:601
  30.1 3.8 %shard_map.71 = (bf16[1024,1024]{1,0:T(8,128)(2,1)S(1)}, bf16[1024,1024]{1,0:T(8,128)(2,1)S(1)}, f32[8,128]{1,0:T(8,128)S(1)}) custom-call(f32[1024,1024]{1,0:T(8,128)S(1)} %get-tuple-element.42.work), custom_call_target="tpu_custom_call" | custom-call | tf_op jit(solution)/shard_map/pallas_call | solution.py:396
  33.9 0.7 shard_map.72.own_ref
  34.6 2.6 %collective-permute-done.4.g1 = bf16[1024,128]{1,0:T(8,128)(2,1)S(1)} collective-permute-done((bf16[1024,128]{1,0:T(8,128)(2,1)S(1)}, bf16[1024,128]{1,0:T(8,128)(2,1)S(1)}, u32[]{:S(2)}, u32[]{:S(2)}) %collective-permute-start.4) | collective-permute-done | bytes 262176 | tf_op jit(solution)/shard_map/ppermute | solution.py:601
  37.2 2.6 %shard_map.73 = (f32[1024,128]{1,0:T(8,128)S(1)}, f32[1024,128]{1,0:T(8,128)S(1)}, bf16[1024,128]{1,0:T(8,128)(2,1)S(1)}, bf16[1024,128]{1,0:T(8,128)(2,1)S(1)},...) custom-call(s32[1,8]{1,0:T(1,128)S(4)} %get-tuple-element.40.flags, f32[1024,128]{1,0:T(8,128)S(1)} %shard_map.72.own_ref, ...), custom_call_target="tpu_custom_call" | custom-call | tf_op jit(solution)/shard_map/pallas_call | solution.py:656
  39.8 0.7 collective-permute-start.7
  40.5 1.9 %collective-permute-start.8 = (bf16[1024,128]{1,0:T(8,128)(2,1)S(1)}, bf16[1024,128]{1,0:T(8,128)(2,1)S(1)}, u32[]{:S(2)}, u32[]{:S(2)}) collective-permute-start(bf16[1024,128]{1,0:T(8,128)(2,1)S(1)} %get-tuple-element.55), channel_id=1, source_target_pairs={{1,2},{3,4},{5,6},{7,8},{9,10},{11,12},{13,14},{2,1},{4,3},{6,5},{... | collective-permute-start | bytes 786440 | tf_op jit(solution)/shard_map/ppermute | solution.py:601
  42.4 5.5 %collective-permute-start.9 = (bf16[1024,128]{1,0:T(8,128)(2,1)S(1)}, bf16[1024,128]{1,0:T(8,128)(2,1)S(1)}, u32[]{:S(2)}, u32[]{:S(2)}) collective-permute-start(bf16[1024,128]{1,0:T(8,128)(2,1)S(1)} %get-tuple-element.56), channel_id=1, source_target_pairs={{0,16},{16,0},{32,48},{48,32},{64,80},{80,64},{96,112},{112,96},{1... | collective-permute-start | bytes 786440 | tf_op jit(solution)/shard_map/ppermute | solution.py:601
  47.9 0.7 shard_map.74.own_ref
  48.6 0.5 collective-permute-done.8.g1
  49.1 2.5 %collective-permute-done.9.g2 = bf16[1024,128]{1,0:T(8,128)(2,1)S(1)} collective-permute-done((bf16[1024,128]{1,0:T(8,128)(2,1)S(1)}, bf16[1024,128]{1,0:T(8,128)(2,1)S(1)}, u32[]{:S(2)}, u32[]{:S(2)}) %collective-permute-start.9) | collective-permute-done | bytes 262176 | tf_op jit(solution)/shard_map/ppermute | solution.py:601
  51.6 2.5 %shard_map.75 = (f32[1024,128]{1,0:T(8,128)S(1)}, f32[1024,128]{1,0:T(8,128)S(1)}, bf16[1024,128]{1,0:T(8,128)(2,1)S(1)}, bf16[1024,128]{1,0:T(8,128)(2,1)S(1)},...) custom-call(s32[1,8]{1,0:T(1,128)S(4)} %get-tuple-element.40.flags, f32[1024,128]{1,0:T(8,128)S(1)} %shard_map.74.own_ref, ...), custom_call_target="tpu_custom_call" | custom-call | tf_op jit(solution)/shard_map/pallas_call | solution.py:656
  54.2 0.7 collective-permute-start.11
  54.9 3.2 %collective-permute-start.12 = (bf16[1024,128]{1,0:T(8,128)(2,1)S(1)}, bf16[1024,128]{1,0:T(8,128)(2,1)S(1)}, u32[]{:S(2)}, u32[]{:S(2)}) collective-permute-start(bf16[1024,128]{1,0:T(8,128)(2,1)S(1)} %get-tuple-element.63), channel_id=1, source_target_pairs={{1,2},{3,4},{5,6},{7,8},{9,10},{11,12},{13,14},{2,1},{4,3},{6,5},{... | collective-permute-start | bytes 786440 | tf_op jit(solution)/shard_map/ppermute | solution.py:601
  58.1 3.4 %collective-permute-start.13 = (bf16[1024,128]{1,0:T(8,128)(2,1)S(1)}, bf16[1024,128]{1,0:T(8,128)(2,1)S(1)}, u32[]{:S(2)}, u32[]{:S(2)}) collective-permute-start(bf16[1024,128]{1,0:T(8,128)(2,1)S(1)} %get-tuple-element.64), channel_id=1, source_target_pairs={{0,16},{16,0},{32,48},{48,32},{64,80},{80,64},{96,112},{112,96},{1... | collective-permute-start | bytes 786440 | tf_op jit(solution)/shard_map/ppermute | solution.py:601
  61.5 1.1 shard_map.76
  62.6 2.7 %collective-permute-done.13.g2 = bf16[1024,128]{1,0:T(8,128)(2,1)S(1)} collective-permute-done((bf16[1024,128]{1,0:T(8,128)(2,1)S(1)}, bf16[1024,128]{1,0:T(8,128)(2,1)S(1)}, u32[]{:S(2)}, u32[]{:S(2)}) %collective-permute-start.13) | collective-permute-done | bytes 262176 | tf_op jit(solution)/shard_map/ppermute | solution.py:601
  65.2 2.1 %shard_map.77 = f32[256,128]{1,0:T(8,128)S(1)} custom-call(s32[1,8]{1,0:T(1,128)S(4)} %get-tuple-element.40.flags, f32[1024,128]{1,0:T(8,128)S(1)} %get-tuple-element.60.own_ref, bf16[1024,1024]{1,0:T(8,128)(2,1)S(1)} %get-tuple-element.45.c_ref, bf16[1024,1024]{1,0:T(8,128)(2,1)S(1)} %get-tuple-element.46.high_ref, ...), custom_call_target="tpu_custom_call" | custom-call | tf_op jit(solution)/shard_map/pallas_call | solution.py:667
  67.3 20.3 %all_to_all.22 = f32[16,16,128]{2,1,0:T(8,128)S(1)} all-to-all(f32[16,16,128]{2,1,0:T(8,128)S(1)} %bitcast.13), channel_id=1, replica_groups={{0,1,16,17,32,33,48,49,64,65,80,81,96,97,112,113},{2,3,18,19,34,35,50,5..., dimensions={0} | all-to-all | bytes 262144 | tf_op jit(solution)/shard_map/all_to_all | solution.py:675
  87.6 0.1 shard_map.78
  87.7 19.9 %all_to_all.23 = f32[16,16,128]{2,1,0:T(8,128)S(1)} all-to-all(f32[16,16,128]{2,1,0:T(8,128)S(1)} %bitcast.11), channel_id=1, replica_groups={{0,2,4,6,8,10,12,14,128,130,132,134,136,138,140,142},{1,3,5,7,9,11,13,1..., dimensions={0} | all-to-all | bytes 262144 | tf_op jit(solution)/shard_map/all_to_all | solution.py:682
  107.6 1.1 shard_map.79
  (12 shorter events, 0.0 us)
Async XLA Ops:
  13.4 7.0 %collective-permute-start.2 = (s32[8,128]{1,0:T(8,128)S(1)}, s32[8,128]{1,0:T(8,128)S(1)}, u32[]{:S(2)}, u32[]{:S(2)}) collective-permute-start(s32[8,128]{1,0:T(8,128)S(1)} %get-tuple-element.35.own), channel_id=1, source_target_pairs={{1,2},{3,4},{5,6},{7,8},{9,10},{11,12},{13,14},{2,1},{4,3},{6,5},{... | collective-permute-start | bytes 12296 | tf_op jit(solution)/shard_map/ppermute | solution.py:609
  17.9 2.7 %collective-permute-start.1 = (s32[8,128]{1,0:T(8,128)S(1)}, s32[8,128]{1,0:T(8,128)S(1)}, u32[]{:S(2)}, u32[]{:S(2)}) collective-permute-start(s32[8,128]{1,0:T(8,128)S(1)} %get-tuple-element.35.own), channel_id=1, source_target_pairs={{0,16},{16,0},{32,48},{48,32},{64,80},{80,64},{96,112},{112,96},{1... | collective-permute-start | bytes 12296 | tf_op jit(solution)/shard_map/ppermute | solution.py:608
  19.7 1.2 %collective-permute-start = (s32[8,128]{1,0:T(8,128)S(1)}, s32[8,128]{1,0:T(8,128)S(1)}, u32[]{:S(2)}, u32[]{:S(2)}) collective-permute-start(s32[8,128]{1,0:T(8,128)S(1)} %get-tuple-element.35.own), channel_id=1, source_target_pairs={{0,1},{1,0},{2,3},{3,2},{4,5},{5,4},{6,7},{7,6},{8,9},{9,8},{10,11... | collective-permute-start | bytes 12296 | tf_op jit(solution)/shard_map/ppermute | solution.py:607
  21.3 13.3 %collective-permute-start.3 = (bf16[1024,128]{1,0:T(8,128)(2,1)S(1)}, bf16[1024,128]{1,0:T(8,128)(2,1)S(1)}, u32[]{:S(2)}, u32[]{:S(2)}) collective-permute-start(bf16[1024,128]{1,0:T(8,128)(2,1)S(1)} %get-tuple-element.48), channel_id=1, source_target_pairs={{16,32},{48,64},{80,96},{112,128},{144,160},{176,192},{208,224},{3... | collective-permute-start | bytes 786440 | tf_op jit(solution)/shard_map/ppermute | solution.py:601
  22.0 15.2 %collective-permute-start.4 = (bf16[1024,128]{1,0:T(8,128)(2,1)S(1)}, bf16[1024,128]{1,0:T(8,128)(2,1)S(1)}, u32[]{:S(2)}, u32[]{:S(2)}) collective-permute-start(bf16[1024,128]{1,0:T(8,128)(2,1)S(1)} %get-tuple-element.49), channel_id=1, source_target_pairs={{1,2},{3,4},{5,6},{7,8},{9,10},{11,12},{13,14},{2,1},{4,3},{6,5},{... | collective-permute-start | bytes 786440 | tf_op jit(solution)/shard_map/ppermute | solution.py:601
  25.2 12.0 %collective-permute-start.5 = (bf16[1024,128]{1,0:T(8,128)(2,1)S(1)}, bf16[1024,128]{1,0:T(8,128)(2,1)S(1)}, u32[]{:S(2)}, u32[]{:S(2)}) collective-permute-start(bf16[1024,128]{1,0:T(8,128)(2,1)S(1)} %get-tuple-element.50), channel_id=1, source_target_pairs={{0,16},{16,0},{32,48},{48,32},{64,80},{80,64},{96,112},{112,96},{1... | collective-permute-start | bytes 786440 | tf_op jit(solution)/shard_map/ppermute | solution.py:601
  30.1 7.1 %collective-permute-start.6 = (bf16[1024,128]{1,0:T(8,128)(2,1)S(1)}, bf16[1024,128]{1,0:T(8,128)(2,1)S(1)}, u32[]{:S(2)}, u32[]{:S(2)}) collective-permute-start(bf16[1024,128]{1,0:T(8,128)(2,1)S(1)} %get-tuple-element.51), channel_id=1, source_target_pairs={{0,1},{1,0},{2,3},{3,2},{4,5},{5,4},{6,7},{7,6},{8,9},{9,8},{10,11... | collective-permute-start | bytes 786440 | tf_op jit(solution)/shard_map/ppermute | solution.py:601
  39.8 8.8 %collective-permute-start.7 = (bf16[1024,128]{1,0:T(8,128)(2,1)S(1)}, bf16[1024,128]{1,0:T(8,128)(2,1)S(1)}, u32[]{:S(2)}, u32[]{:S(2)}) collective-permute-start(bf16[1024,128]{1,0:T(8,128)(2,1)S(1)} %get-tuple-element.54), channel_id=1, source_target_pairs={{16,32},{48,64},{80,96},{112,128},{144,160},{176,192},{208,224},{3... | collective-permute-start | bytes 786440 | tf_op jit(solution)/shard_map/ppermute | solution.py:601
  40.5 8.7 %collective-permute-start.8 = (bf16[1024,128]{1,0:T(8,128)(2,1)S(1)}, bf16[1024,128]{1,0:T(8,128)(2,1)S(1)}, u32[]{:S(2)}, u32[]{:S(2)}) collective-permute-start(bf16[1024,128]{1,0:T(8,128)(2,1)S(1)} %get-tuple-element.55), channel_id=1, source_target_pairs={{1,2},{3,4},{5,6},{7,8},{9,10},{11,12},{13,14},{2,1},{4,3},{6,5},{... | collective-permute-start | bytes 786440 | tf_op jit(solution)/shard_map/ppermute | solution.py:601
  42.4 9.2 %collective-permute-start.9 = (bf16[1024,128]{1,0:T(8,128)(2,1)S(1)}, bf16[1024,128]{1,0:T(8,128)(2,1)S(1)}, u32[]{:S(2)}, u32[]{:S(2)}) collective-permute-start(bf16[1024,128]{1,0:T(8,128)(2,1)S(1)} %get-tuple-element.56), channel_id=1, source_target_pairs={{0,16},{16,0},{32,48},{48,32},{64,80},{80,64},{96,112},{112,96},{1... | collective-permute-start | bytes 786440 | tf_op jit(solution)/shard_map/ppermute | solution.py:601
  47.9 3.8 %collective-permute-start.10 = (bf16[1024,128]{1,0:T(8,128)(2,1)S(1)}, bf16[1024,128]{1,0:T(8,128)(2,1)S(1)}, u32[]{:S(2)}, u32[]{:S(2)}) collective-permute-start(bf16[1024,128]{1,0:T(8,128)(2,1)S(1)} %get-tuple-element.57), channel_id=1, source_target_pairs={{0,1},{1,0},{2,3},{3,2},{4,5},{5,4},{6,7},{7,6},{8,9},{9,8},{10,11... | collective-permute-start | bytes 786440 | tf_op jit(solution)/shard_map/ppermute | solution.py:601
  54.2 8.4 %collective-permute-start.11 = (bf16[1024,128]{1,0:T(8,128)(2,1)S(1)}, bf16[1024,128]{1,0:T(8,128)(2,1)S(1)}, u32[]{:S(2)}, u32[]{:S(2)}) collective-permute-start(bf16[1024,128]{1,0:T(8,128)(2,1)S(1)} %get-tuple-element.62), channel_id=1, source_target_pairs={{16,32},{48,64},{80,96},{112,128},{144,160},{176,192},{208,224},{3... | collective-permute-start | bytes 786440 | tf_op jit(solution)/shard_map/ppermute | solution.py:601
  54.9 7.7 %collective-permute-start.12 = (bf16[1024,128]{1,0:T(8,128)(2,1)S(1)}, bf16[1024,128]{1,0:T(8,128)(2,1)S(1)}, u32[]{:S(2)}, u32[]{:S(2)}) collective-permute-start(bf16[1024,128]{1,0:T(8,128)(2,1)S(1)} %get-tuple-element.63), channel_id=1, source_target_pairs={{1,2},{3,4},{5,6},{7,8},{9,10},{11,12},{13,14},{2,1},{4,3},{6,5},{... | collective-permute-start | bytes 786440 | tf_op jit(solution)/shard_map/ppermute | solution.py:601
  58.1 7.1 %collective-permute-start.13 = (bf16[1024,128]{1,0:T(8,128)(2,1)S(1)}, bf16[1024,128]{1,0:T(8,128)(2,1)S(1)}, u32[]{:S(2)}, u32[]{:S(2)}) collective-permute-start(bf16[1024,128]{1,0:T(8,128)(2,1)S(1)} %get-tuple-element.64), channel_id=1, source_target_pairs={{0,16},{16,0},{32,48},{48,32},{64,80},{80,64},{96,112},{112,96},{1... | collective-permute-start | bytes 786440 | tf_op jit(solution)/shard_map/ppermute | solution.py:601
  61.5 3.8 %collective-permute-start.14 = (bf16[1024,128]{1,0:T(8,128)(2,1)S(1)}, bf16[1024,128]{1,0:T(8,128)(2,1)S(1)}, u32[]{:S(2)}, u32[]{:S(2)}) collective-permute-start(bf16[1024,128]{1,0:T(8,128)(2,1)S(1)} %get-tuple-element.65), channel_id=1, source_target_pairs={{0,1},{1,0},{2,3},{3,2},{4,5},{5,4},{6,7},{7,6},{8,9},{9,8},{10,11... | collective-permute-start | bytes 786440 | tf_op jit(solution)/shard_map/ppermute | solution.py:601

commit v5 on v4

--- a/solution.py
+++ b/solution.py
@@ -331,7 +331,7 @@
         back[rows, :] = mm(ct_ref[rows, :], high).astype(BF16)
 
 
-def message_kernel(last, t3, t2, t1, own, ahead, back, flags, m0, m1, m2, m3):
+def message_kernel(last, t3, t1, t2, own, ahead, back, flags, m0, m1, m2, m3):
     here, *times = [jnp.max(t[...]) for t in (own, t1, t2, t3)]
     next_left = here < last
     prev_left = here > 1
@@ -364,7 +364,7 @@
         in_specs=[vmem()] * 6,
         out_specs=[smem()] + [vmem()] * 4,
         compiler_params=params(8),
-    )(*[pinned(t) for t in reversed(tags)], *[pinned(p) for p in parts])
+    )(*[pinned(tags[i]) for i in (3, 1, 2, 0)], *[pinned(p) for p in parts])
 
 
 def build_kernel(work, high_ref, low_ref, size_ref):
@@ -597,7 +597,7 @@
 def exchange(values):
     even_r, odd_r = neighbour_perms(lax.axis_size("tr"))
     even_c, odd_c = neighbour_perms(lax.axis_size("tc"))
-    routes = (("tr", odd_r), ("tc", odd_c), ("tr", even_r), ("tc", even_c))
+    routes = (("tr", odd_r), ("tr", even_r), ("tc", odd_c), ("tc", even_c))
     return [lax.ppermute(v, *route) for v, route in zip(values, routes)]
 
 
@@ -606,19 +606,7 @@
     even_c, odd_c = neighbour_perms(lax.axis_size("tc"))
     near = lax.ppermute(tag, "tc", even_c)
     below = lax.ppermute(tag, "tr", even_r)
-    return [lax.ppermute(tag, "tc", odd_c), below, near]
-
-
-def reduce_groups():
-    rows, cols = lax.axis_size("tr"), lax.axis_size("tc")
-    deep = rows // 2
-
-    def rank(h, z, q, c):
-        return (h * deep + z) * cols + q * 2 + c
-
-    lines = [[rank(h, z, q, c) for z in range(deep) for c in range(2)] for h in range(2) for q in range(cols // 2)]
-    planes = [[rank(h, z, q, c) for h in range(2) for q in range(cols // 2)] for z in range(deep) for c in range(2)]
-    return lines, planes
+    return [below, lax.ppermute(tag, "tc", odd_c), near]
 
 
 def body(diag_block, coupling, precond, rhs, slot_time):
@@ -663,23 +651,22 @@
             vec = out[1]
             basis += [out[0], vec]
             messages = out[2:]
-    lines, planes = reduce_groups()
     part = pl.pallas_call(
         last_kernel,
-        out_shape=pltpu.VMEM((len(lines[0]) * SLOTS, width), F32),
+        out_shape=pltpu.VMEM((lax.axis_size("tc") * SLOTS, width), F32),
         in_specs=[smem()] + [vmem()] * 13,
         out_specs=vmem(),
         scratch_shapes=[pltpu.VMEM((n, width), F32)] * 2,
         compiler_params=params(12),
     )(pinned(flags, pltpu.SMEM), pinned(own), pinned(c_here), pinned(high), pinned(low), pinned(size), pinned(early), *[pinned(b) for b in basis[::2]], *got)
-    part = lax.all_to_all(part, ("tr", "tc"), 0, 0, tiled=True, axis_index_groups=lines)
+    part = lax.all_to_all(part, "tc", 0, 0, tiled=True)
     part = pl.pallas_call(
         merge_kernel,
-        out_shape=pltpu.VMEM((len(planes[0]) * SLOTS, width), F32),
+        out_shape=pltpu.VMEM((lax.axis_size("tr") * SLOTS, width), F32),
         in_specs=[vmem()],
         out_specs=vmem(),
     )(pinned(part))
-    part = lax.all_to_all(part, ("tr", "tc"), 0, 0, tiled=True, axis_index_groups=planes)
+    part = lax.all_to_all(part, "tr", 0, 0, tiled=True)
     solution, norm = pl.pallas_call(
         finish_kernel,
         out_shape=[jax.ShapeDtypeStruct((n, width), F32), jax.ShapeDtypeStruct((1, width), F32)],

time: 109 us -> 107 us (0.982)
  waiting for transfers between devices: 8.75 us -> 28.7 us
  blocking collectives: 40.2 us -> 25.8 us
  starting transfers between devices: 30.4 us -> 22.9 us
    ppermute x12, waiting for transfers between devices: 8.3 us -> 28.2 us  [exchange(): return [lax.ppermute(v, *route) for v, route in zip(values, routes)]]
    all_to_all x2, blocking collectives: 40.2 us -> 25.8 us  [the longest x1 13 us: body(): part = lax.all_to_all(part, 'tr', 0, 0, tiled=True)]
    ppermute x12, starting transfers between devices: 24.1 us -> 16.6 us  [exchange(): return [lax.ppermute(v, *route) for v, route in zip(values, routes)]]
  transfers between devices with their start and end apart: 15 -> 15, of which waited for: 6 -> 7; matrix products, arithmetic and copies ran while one was open for 0% -> 0% of each run, Pallas kernels for 6% -> 7%
where the time goes in v5:
time: 107 us
  waiting for transfers between devices  28.7 us (27%)
  Pallas kernels  27.9 us (26%)
  blocking collectives  25.8 us (24%)
  starting transfers between devices  22.9 us (21%)
  between operations  1.49 us (1%)
    ppermute x12, waiting for transfers between devices, exchange(): return [lax.ppermute(v, *route) for v, route in zip(values, routes)]  28.2 us
    ppermute x12, starting transfers between devices, exchange(): return [lax.ppermute(v, *route) for v, route in zip(values, routes)]  16.6 us
    all_to_all x1, blocking collectives, body(): part = lax.all_to_all(part, 'tr', 0, 0, tiled=True)  13 us
    all_to_all x1, blocking collectives, body(): part = lax.all_to_all(part, 'tc', 0, 0, tiled=True)  12.8 us
    pallas_call x1, Pallas kernels, factor(): pl.pallas_call(factor_kernel, out_shape=[pltpu.VMEM((n, n), F32), square,...  12.1 us
    pallas_call x2, Pallas kernels, body(): pl.pallas_call(step_kernel, out_shape=[pltpu.VMEM((n, width), F32)] * 2 +...  5.08 us
    ppermute x1, starting transfers between devices, exchange_tags(): return [below, lax.ppermute(tag, 'tc', odd_c), near]  4.51 us
    pallas_call x1, Pallas kernels, build(): pl.pallas_call(build_kernel, out_shape=[pltpu.VMEM((n, n), BF16), pltpu.V...  3.8 us
  transfers between devices with their start and end apart: 15, of which 7 were waited for; matrix products, arithmetic and copies ran while one was open for 0% of the time, Pallas kernels for 7%

profile of v5, /device:TPU:1, one launch (start us, length us, event | category | flops | bytes accessed | tf_op | source)
XLA Modules:
  0.0 106.8 jit_solution(9453539060959838751)
XLA Ops:
  1.3 12.1 %shard_map.68 = (f32[1024,1024]{1,0:T(8,128)S(1)}, bf16[1024,1024]{1,0:T(8,128)(2,1)S(1)}, bf16[1024,1024]{1,0:T(8,128)(2,1)S(1)}, bf16[1024,1024]{1,0:T(8,128)(...) custom-call(s32[1,1]{1,0:T(1,128)S(6)} %copy.7.time, f32[1024,1024]{1,0:T(8,128)} %bitcast.14, ...), custom_call_target="tpu_custom_call" | custom-call | tf_op jit(solution)/shard_map/pallas_call | solution.py:316
  13.4 4.5 %collective-permute-start.2 = (s32[8,128]{1,0:T(8,128)S(1)}, s32[8,128]{1,0:T(8,128)S(1)}, u32[]{:S(2)}, u32[]{:S(2)}) collective-permute-start(s32[8,128]{1,0:T(8,128)S(1)} %get-tuple-element.35.own), channel_id=1, source_target_pairs={{1,2},{3,4},{5,6},{7,8},{9,10},{11,12},{13,14},{2,1},{4,3},{6,5},{... | collective-permute-start | bytes 12296 | tf_op jit(solution)/shard_map/ppermute | solution.py:609
  17.9 1.7 %collective-permute-start.1 = (s32[8,128]{1,0:T(8,128)S(1)}, s32[8,128]{1,0:T(8,128)S(1)}, u32[]{:S(2)}, u32[]{:S(2)}) collective-permute-start(s32[8,128]{1,0:T(8,128)S(1)} %get-tuple-element.35.own), channel_id=1, source_target_pairs={{0,16},{16,0},{32,48},{48,32},{64,80},{80,64},{96,112},{112,96},{1... | collective-permute-start | bytes 12296 | tf_op jit(solution)/shard_map/ppermute | solution.py:608
  19.7 0.7 shard_map.69
  20.4 0.3 collective-permute-done.1.t1
  20.7 0.2 collective-permute-done.t3
  20.8 0.5 shard_map.70
  21.3 0.7 collective-permute-start.3
  22.0 4.6 %collective-permute-start.4 = (bf16[1024,128]{1,0:T(8,128)(2,1)S(1)}, bf16[1024,128]{1,0:T(8,128)(2,1)S(1)}, u32[]{:S(2)}, u32[]{:S(2)}) collective-permute-start(bf16[1024,128]{1,0:T(8,128)(2,1)S(1)} %get-tuple-element.49), channel_id=1, source_target_pairs={{0,16},{16,0},{32,48},{48,32},{64,80},{80,64},{96,112},{112,96},{1... | collective-permute-start | bytes 786440 | tf_op jit(solution)/shard_map/ppermute | solution.py:601
  26.6 3.8 %collective-permute-start.5 = (bf16[1024,128]{1,0:T(8,128)(2,1)S(1)}, bf16[1024,128]{1,0:T(8,128)(2,1)S(1)}, u32[]{:S(2)}, u32[]{:S(2)}) collective-permute-start(bf16[1024,128]{1,0:T(8,128)(2,1)S(1)} %get-tuple-element.50), channel_id=1, source_target_pairs={{1,2},{3,4},{5,6},{7,8},{9,10},{11,12},{13,14},{2,1},{4,3},{6,5},{... | collective-permute-start | bytes 786440 | tf_op jit(solution)/shard_map/ppermute | solution.py:601
  30.5 3.8 %shard_map.71 = (bf16[1024,1024]{1,0:T(8,128)(2,1)S(1)}, bf16[1024,1024]{1,0:T(8,128)(2,1)S(1)}, f32[8,128]{1,0:T(8,128)S(1)}) custom-call(f32[1024,1024]{1,0:T(8,128)S(1)} %get-tuple-element.42.work), custom_call_target="tpu_custom_call" | custom-call | tf_op jit(solution)/shard_map/pallas_call | solution.py:396
  34.3 0.7 shard_map.72.own_ref
  35.0 6.5 %collective-permute-done.5.g2 = bf16[1024,128]{1,0:T(8,128)(2,1)S(1)} collective-permute-done((bf16[1024,128]{1,0:T(8,128)(2,1)S(1)}, bf16[1024,128]{1,0:T(8,128)(2,1)S(1)}, u32[]{:S(2)}, u32[]{:S(2)}) %collective-permute-start.5) | collective-permute-done | bytes 262176 | tf_op jit(solution)/shard_map/ppermute | solution.py:601
  41.5 2.6 %shard_map.73 = (f32[1024,128]{1,0:T(8,128)S(1)}, f32[1024,128]{1,0:T(8,128)S(1)}, bf16[1024,128]{1,0:T(8,128)(2,1)S(1)}, bf16[1024,128]{1,0:T(8,128)(2,1)S(1)},...) custom-call(s32[1,8]{1,0:T(1,128)S(4)} %get-tuple-element.40.flags, f32[1024,128]{1,0:T(8,128)S(1)} %shard_map.72.own_ref, ...), custom_call_target="tpu_custom_call" | custom-call | tf_op jit(solution)/shard_map/pallas_call | solution.py:644
  44.1 0.7 collective-permute-start.7
  44.8 0.1 collective-permute-start.8
  44.9 3.6 %collective-permute-start.9 = (bf16[1024,128]{1,0:T(8,128)(2,1)S(1)}, bf16[1024,128]{1,0:T(8,128)(2,1)S(1)}, u32[]{:S(2)}, u32[]{:S(2)}) collective-permute-start(bf16[1024,128]{1,0:T(8,128)(2,1)S(1)} %get-tuple-element.56), channel_id=1, source_target_pairs={{1,2},{3,4},{5,6},{7,8},{9,10},{11,12},{13,14},{2,1},{4,3},{6,5},{... | collective-permute-start | bytes 786440 | tf_op jit(solution)/shard_map/ppermute | solution.py:601
  48.5 0.3 collective-permute-start.10
  48.8 0.7 shard_map.74.own_ref
  49.6 1.6 %collective-permute-done.8.g1 = bf16[1024,128]{1,0:T(8,128)(2,1)S(1)} collective-permute-done((bf16[1024,128]{1,0:T(8,128)(2,1)S(1)}, bf16[1024,128]{1,0:T(8,128)(2,1)S(1)}, u32[]{:S(2)}, u32[]{:S(2)}) %collective-permute-start.8) | collective-permute-done | bytes 262176 | tf_op jit(solution)/shard_map/ppermute | solution.py:601
  51.1 9.5 %collective-permute-done.9.g2 = bf16[1024,128]{1,0:T(8,128)(2,1)S(1)} collective-permute-done((bf16[1024,128]{1,0:T(8,128)(2,1)S(1)}, bf16[1024,128]{1,0:T(8,128)(2,1)S(1)}, u32[]{:S(2)}, u32[]{:S(2)}) %collective-permute-start.9) | collective-permute-done | bytes 262176 | tf_op jit(solution)/shard_map/ppermute | solution.py:601
  60.6 2.5 %shard_map.75 = (f32[1024,128]{1,0:T(8,128)S(1)}, f32[1024,128]{1,0:T(8,128)S(1)}, bf16[1024,128]{1,0:T(8,128)(2,1)S(1)}, bf16[1024,128]{1,0:T(8,128)(2,1)S(1)},...) custom-call(s32[1,8]{1,0:T(1,128)S(4)} %get-tuple-element.40.flags, f32[1024,128]{1,0:T(8,128)S(1)} %shard_map.74.own_ref, ...), custom_call_target="tpu_custom_call" | custom-call | tf_op jit(solution)/shard_map/pallas_call | solution.py:644
  63.2 0.7 collective-permute-start.11
  63.8 0.1 collective-permute-start.12
  63.9 1.9 %collective-permute-start.13 = (bf16[1024,128]{1,0:T(8,128)(2,1)S(1)}, bf16[1024,128]{1,0:T(8,128)(2,1)S(1)}, u32[]{:S(2)}, u32[]{:S(2)}) collective-permute-start(bf16[1024,128]{1,0:T(8,128)(2,1)S(1)} %get-tuple-element.64), channel_id=1, source_target_pairs={{1,2},{3,4},{5,6},{7,8},{9,10},{11,12},{13,14},{2,1},{4,3},{6,5},{... | collective-permute-start | bytes 786440 | tf_op jit(solution)/shard_map/ppermute | solution.py:601
  66.0 1.1 %shard_map.76 = (f32[1024,128]{1,0:T(8,128)S(1)}, f32[16,128]{1,0:T(8,128)S(1)}) custom-call(bf16[1024,1024]{1,0:T(8,128)(2,1)S(1)} %get-tuple-element.41.diag_ref, f32[8,128]{1,0:T(8,128)S(1)} %get-tuple-element.43.size_ref, f32[1024,128]{1,0:T(8,128)S(1)} %get-tuple-element.44.r0, f32[1024,128]{1,0:T(8,128)S(1)} %get-tuple-element.37.vec_ref.p0, ...), custom_call_target="tpu_custom_call" | custom-call | tf_op jit(solution)/shard_map/pallas_call | solution.py:636
  67.1 2.1 %collective-permute-done.12.g1 = bf16[1024,128]{1,0:T(8,128)(2,1)S(1)} collective-permute-done((bf16[1024,128]{1,0:T(8,128)(2,1)S(1)}, bf16[1024,128]{1,0:T(8,128)(2,1)S(1)}, u32[]{:S(2)}, u32[]{:S(2)}) %collective-permute-start.12) | collective-permute-done | bytes 262176 | tf_op jit(solution)/shard_map/ppermute | solution.py:601
  69.2 8.6 %collective-permute-done.13.g2 = bf16[1024,128]{1,0:T(8,128)(2,1)S(1)} collective-permute-done((bf16[1024,128]{1,0:T(8,128)(2,1)S(1)}, bf16[1024,128]{1,0:T(8,128)(2,1)S(1)}, u32[]{:S(2)}, u32[]{:S(2)}) %collective-permute-start.13) | collective-permute-done | bytes 262176 | tf_op jit(solution)/shard_map/ppermute | solution.py:601
  77.7 2.1 %shard_map.77 = f32[256,128]{1,0:T(8,128)S(1)} custom-call(s32[1,8]{1,0:T(1,128)S(4)} %get-tuple-element.40.flags, f32[1024,128]{1,0:T(8,128)S(1)} %get-tuple-element.60.own_ref, bf16[1024,1024]{1,0:T(8,128)(2,1)S(1)} %get-tuple-element.45.c_ref, bf16[1024,1024]{1,0:T(8,128)(2,1)S(1)} %get-tuple-element.46.high_ref, ...), custom_call_target="tpu_custom_call" | custom-call | tf_op jit(solution)/shard_map/pallas_call | solution.py:654
  79.8 12.8 %all_to_all.22 = f32[16,16,128]{2,1,0:T(8,128)S(1)} all-to-all(f32[16,16,128]{2,1,0:T(8,128)S(1)} %bitcast.13), channel_id=1, replica_groups=mesh['tr'=16,'tc'=16] {'tc'}, dimensions={0} | all-to-all | bytes 262144 | tf_op jit(solution)/shard_map/all_to_all | solution.py:662
  92.7 13.0 %all_to_all.23 = f32[16,16,128]{2,1,0:T(8,128)S(1)} all-to-all(f32[16,16,128]{2,1,0:T(8,128)S(1)} %bitcast.11), channel_id=1, replica_groups=mesh['tr'=16,'tc'=16] {'tr'}, dimensions={0} | all-to-all | bytes 262144 | tf_op jit(solution)/shard_map/all_to_all | solution.py:669
  105.7 1.1 shard_map.79
  (12 shorter events, 0.3 us)
Async XLA Ops:
  13.4 7.0 %collective-permute-start.2 = (s32[8,128]{1,0:T(8,128)S(1)}, s32[8,128]{1,0:T(8,128)S(1)}, u32[]{:S(2)}, u32[]{:S(2)}) collective-permute-start(s32[8,128]{1,0:T(8,128)S(1)} %get-tuple-element.35.own), channel_id=1, source_target_pairs={{1,2},{3,4},{5,6},{7,8},{9,10},{11,12},{13,14},{2,1},{4,3},{6,5},{... | collective-permute-start | bytes 12296 | tf_op jit(solution)/shard_map/ppermute | solution.py:609
  17.9 2.7 %collective-permute-start.1 = (s32[8,128]{1,0:T(8,128)S(1)}, s32[8,128]{1,0:T(8,128)S(1)}, u32[]{:S(2)}, u32[]{:S(2)}) collective-permute-start(s32[8,128]{1,0:T(8,128)S(1)} %get-tuple-element.35.own), channel_id=1, source_target_pairs={{0,16},{16,0},{32,48},{48,32},{64,80},{80,64},{96,112},{112,96},{1... | collective-permute-start | bytes 12296 | tf_op jit(solution)/shard_map/ppermute | solution.py:608
  19.7 1.2 %collective-permute-start = (s32[8,128]{1,0:T(8,128)S(1)}, s32[8,128]{1,0:T(8,128)S(1)}, u32[]{:S(2)}, u32[]{:S(2)}) collective-permute-start(s32[8,128]{1,0:T(8,128)S(1)} %get-tuple-element.35.own), channel_id=1, source_target_pairs={{0,1},{1,0},{2,3},{3,2},{4,5},{5,4},{6,7},{7,6},{8,9},{9,8},{10,11... | collective-permute-start | bytes 12296 | tf_op jit(solution)/shard_map/ppermute | solution.py:607
  21.3 13.7 %collective-permute-start.3 = (bf16[1024,128]{1,0:T(8,128)(2,1)S(1)}, bf16[1024,128]{1,0:T(8,128)(2,1)S(1)}, u32[]{:S(2)}, u32[]{:S(2)}) collective-permute-start(bf16[1024,128]{1,0:T(8,128)(2,1)S(1)} %get-tuple-element.48), channel_id=1, source_target_pairs={{16,32},{48,64},{80,96},{112,128},{144,160},{176,192},{208,224},{3... | collective-permute-start | bytes 786440 | tf_op jit(solution)/shard_map/ppermute | solution.py:601
  22.0 13.0 %collective-permute-start.4 = (bf16[1024,128]{1,0:T(8,128)(2,1)S(1)}, bf16[1024,128]{1,0:T(8,128)(2,1)S(1)}, u32[]{:S(2)}, u32[]{:S(2)}) collective-permute-start(bf16[1024,128]{1,0:T(8,128)(2,1)S(1)} %get-tuple-element.49), channel_id=1, source_target_pairs={{0,16},{16,0},{32,48},{48,32},{64,80},{80,64},{96,112},{112,96},{1... | collective-permute-start | bytes 786440 | tf_op jit(solution)/shard_map/ppermute | solution.py:601
  26.6 14.9 %collective-permute-start.5 = (bf16[1024,128]{1,0:T(8,128)(2,1)S(1)}, bf16[1024,128]{1,0:T(8,128)(2,1)S(1)}, u32[]{:S(2)}, u32[]{:S(2)}) collective-permute-start(bf16[1024,128]{1,0:T(8,128)(2,1)S(1)} %get-tuple-element.50), channel_id=1, source_target_pairs={{1,2},{3,4},{5,6},{7,8},{9,10},{11,12},{13,14},{2,1},{4,3},{6,5},{... | collective-permute-start | bytes 786440 | tf_op jit(solution)/shard_map/ppermute | solution.py:601
  30.4 11.1 %collective-permute-start.6 = (bf16[1024,128]{1,0:T(8,128)(2,1)S(1)}, bf16[1024,128]{1,0:T(8,128)(2,1)S(1)}, u32[]{:S(2)}, u32[]{:S(2)}) collective-permute-start(bf16[1024,128]{1,0:T(8,128)(2,1)S(1)} %get-tuple-element.51), channel_id=1, source_target_pairs={{0,1},{1,0},{2,3},{3,2},{4,5},{5,4},{6,7},{7,6},{8,9},{9,8},{10,11... | collective-permute-start | bytes 786440 | tf_op jit(solution)/shard_map/ppermute | solution.py:601
  44.1 5.5 %collective-permute-start.7 = (bf16[1024,128]{1,0:T(8,128)(2,1)S(1)}, bf16[1024,128]{1,0:T(8,128)(2,1)S(1)}, u32[]{:S(2)}, u32[]{:S(2)}) collective-permute-start(bf16[1024,128]{1,0:T(8,128)(2,1)S(1)} %get-tuple-element.54), channel_id=1, source_target_pairs={{16,32},{48,64},{80,96},{112,128},{144,160},{176,192},{208,224},{3... | collective-permute-start | bytes 786440 | tf_op jit(solution)/shard_map/ppermute | solution.py:601
  44.8 6.4 %collective-permute-start.8 = (bf16[1024,128]{1,0:T(8,128)(2,1)S(1)}, bf16[1024,128]{1,0:T(8,128)(2,1)S(1)}, u32[]{:S(2)}, u32[]{:S(2)}) collective-permute-start(bf16[1024,128]{1,0:T(8,128)(2,1)S(1)} %get-tuple-element.55), channel_id=1, source_target_pairs={{0,16},{16,0},{32,48},{48,32},{64,80},{80,64},{96,112},{112,96},{1... | collective-permute-start | bytes 786440 | tf_op jit(solution)/shard_map/ppermute | solution.py:601
  44.9 15.8 %collective-permute-start.9 = (bf16[1024,128]{1,0:T(8,128)(2,1)S(1)}, bf16[1024,128]{1,0:T(8,128)(2,1)S(1)}, u32[]{:S(2)}, u32[]{:S(2)}) collective-permute-start(bf16[1024,128]{1,0:T(8,128)(2,1)S(1)} %get-tuple-element.56), channel_id=1, source_target_pairs={{1,2},{3,4},{5,6},{7,8},{9,10},{11,12},{13,14},{2,1},{4,3},{6,5},{... | collective-permute-start | bytes 786440 | tf_op jit(solution)/shard_map/ppermute | solution.py:601
  48.5 12.1 %collective-permute-start.10 = (bf16[1024,128]{1,0:T(8,128)(2,1)S(1)}, bf16[1024,128]{1,0:T(8,128)(2,1)S(1)}, u32[]{:S(2)}, u32[]{:S(2)}) collective-permute-start(bf16[1024,128]{1,0:T(8,128)(2,1)S(1)} %get-tuple-element.57), channel_id=1, source_target_pairs={{0,1},{1,0},{2,3},{3,2},{4,5},{5,4},{6,7},{7,6},{8,9},{9,8},{10,11... | collective-permute-start | bytes 786440 | tf_op jit(solution)/shard_map/ppermute | solution.py:601
  63.2 3.9 %collective-permute-start.11 = (bf16[1024,128]{1,0:T(8,128)(2,1)S(1)}, bf16[1024,128]{1,0:T(8,128)(2,1)S(1)}, u32[]{:S(2)}, u32[]{:S(2)}) collective-permute-start(bf16[1024,128]{1,0:T(8,128)(2,1)S(1)} %get-tuple-element.62), channel_id=1, source_target_pairs={{16,32},{48,64},{80,96},{112,128},{144,160},{176,192},{208,224},{3... | collective-permute-start | bytes 786440 | tf_op jit(solution)/shard_map/ppermute | solution.py:601
  63.8 5.3 %collective-permute-start.12 = (bf16[1024,128]{1,0:T(8,128)(2,1)S(1)}, bf16[1024,128]{1,0:T(8,128)(2,1)S(1)}, u32[]{:S(2)}, u32[]{:S(2)}) collective-permute-start(bf16[1024,128]{1,0:T(8,128)(2,1)S(1)} %get-tuple-element.63), channel_id=1, source_target_pairs={{0,16},{16,0},{32,48},{48,32},{64,80},{80,64},{96,112},{112,96},{1... | collective-permute-start | bytes 786440 | tf_op jit(solution)/shard_map/ppermute | solution.py:601
  63.9 13.8 %collective-permute-start.13 = (bf16[1024,128]{1,0:T(8,128)(2,1)S(1)}, bf16[1024,128]{1,0:T(8,128)(2,1)S(1)}, u32[]{:S(2)}, u32[]{:S(2)}) collective-permute-start(bf16[1024,128]{1,0:T(8,128)(2,1)S(1)} %get-tuple-element.64), channel_id=1, source_target_pairs={{1,2},{3,4},{5,6},{7,8},{9,10},{11,12},{13,14},{2,1},{4,3},{6,5},{... | collective-permute-start | bytes 786440 | tf_op jit(solution)/shard_map/ppermute | solution.py:601
  65.9 11.9 %collective-permute-start.14 = (bf16[1024,128]{1,0:T(8,128)(2,1)S(1)}, bf16[1024,128]{1,0:T(8,128)(2,1)S(1)}, u32[]{:S(2)}, u32[]{:S(2)}) collective-permute-start(bf16[1024,128]{1,0:T(8,128)(2,1)S(1)} %get-tuple-element.65), channel_id=1, source_target_pairs={{0,1},{1,0},{2,3},{3,2},{4,5},{5,4},{6,7},{7,6},{8,9},{9,8},{10,11... | collective-permute-start | bytes 786440 | tf_op jit(solution)/shard_map/ppermute | solution.py:601
